TPU v7x, 32 devices: a whole 2x2x4 slice. The times are simulated.
32 devices in a mesh: tm: 4 (over y, x), region: 8 (over z, core).
Axes of the slice: x: 2, y: 2, z: 4, core: 2. Of those that a mesh axis runs over, the one named last changes fastest.
Arguments:
- search_one: float32 [4, 548, 8192], P('tm', None, 'region'), may hold values from -6 to 6
- search_two: float32 [4, 548, 8192], P('tm', None, 'region'), may hold values from -6 to 6
- column_gain: float32 [4, 548, 8192], P('tm', None, 'region'), may hold values from 0.5 to 1.25
- model_matrix: float32 [4, 548, 548], P('tm'), may hold values from -0.25 to 0.25
- obs_owner: int32 [4, 8192], P('tm', 'region'), may hold values from 0 to 7, as said below
- observe_matrix: float32 [4, 8, 548, 1024], P('tm', 'region'), may hold values from -0.25 to 0.25
- error_weight: float32 [4, 8, 1024], P('tm', 'region'), may hold values from 0.25 to 4
- channel_mask: int32 [4, 8, 1024], P('tm', 'region'), may hold values 0 or 1
Outputs:
- forward_state: float32 [4, 548, 8192], P('tm', None, 'region')
- gradient: float32 [4, 548, 8192], P('tm', None, 'region')
Inputs may be any that keep to these rules, and one draw needn't show every extreme that they name: `obs_owner`: among the 1024 columns of one device (one subwindow, one aligned block of 1024 columns) no owner appears more than 192 times; in every subwindow one owner appears exactly 192 times in every block.
All inputs are finite; a program needn't handle non-finite values. No bound on the sum of `channel_mask` on one device may be relied on, other than what follows from the above.
Results may differ from a plain program's by a relative error of at most 0.0003.
Values sent between devices are 32-bit elements; how exact they have to be, the bound alone decides.
No kernel may reach another device: no remote copies, remote signals or barrier semaphores. Data moves between devices by JAX's collectives and lax.ppermute only.
A program may use at most 128 MiB of HBM per device.

v0:
```python
import functools

import jax
import jax.numpy as jnp
from jax import lax
from jax.experimental import pallas as pl
from jax.experimental.pallas import tpu as pltpu
from jax.sharding import PartitionSpec as P

LANES = 128
F32 = jnp.float32
BF16 = jnp.bfloat16
WHOLE = pl.BlockSpec(memory_space=pltpu.VMEM)
ANY = pl.BlockSpec(memory_space=pl.ANY)
HBM = pl.BlockSpec(memory_space=pltpu.HBM)


def far(x):
    return pltpu.with_memory_space_constraint(x, pltpu.HBM)


def near(x):
    return pltpu.with_memory_space_constraint(x, pltpu.VMEM)


def params(mebibytes):
    return pltpu.CompilerParams(vmem_limit_bytes=mebibytes * 1024 * 1024)


def cost(flops, touched):
    return pl.CostEstimate(flops=int(flops), bytes_accessed=int(touched), transcendentals=0)


def up(size, to):
    return -(-size // to) * to


def split(x):
    high = x.astype(BF16)
    return high, (x - high.astype(F32)).astype(BF16)


def dot(left, right):
    return jnp.dot(left, right, preferred_element_type=F32)


def stacking(size):
    main = size // LANES * LANES
    rest = size - main
    return main, rest, up(rest, 16)


def stacked(size):
    main, _, room = stacking(size)
    return 3 * (main + room)


def stack_left(ref, matrix):
    main, rest, room = stacking(matrix.shape[1])
    if room > rest:
        ref[:, 3 * main :] = jnp.zeros((matrix.shape[0], 3 * room), BF16)
    for k, term in enumerate(split(matrix)):
        for at in (0, 1) if k == 0 else (2,):
            ref[:, at * main : (at + 1) * main] = term[:, 0:main]
            if rest:
                start = 3 * main + at * room
                ref[:, start : start + rest] = term[:, main : main + rest]


def stack_right(ref, x):
    main, rest, room = stacking(x.shape[0])
    for k, term in enumerate(split(x)):
        end = term[main : main + rest, :]
        if room > rest:
            end = jnp.concatenate([end, jnp.zeros((room - rest, x.shape[1]), BF16)], axis=0)
        for at in (0, 2) if k == 0 else (1,):
            ref[at * main : (at + 1) * main, :] = term[0:main, :]
            if rest:
                start = 3 * main + at * room
                ref[start : start + room, :] = end


def columns_of(source, width, piece):
    return source.at[:, 0, piece * width : (piece + 1) * width]


def load(copies):
    for copy in copies:
        copy.start()
    for copy in copies:
        copy.wait()


def packing(size):
    half = size // (2 * LANES) * LANES
    rest = size - 2 * half
    cell = LANES // 2 if rest <= LANES // 2 else LANES
    across = 2 * half // cell
    strip = half
    corner = strip + up(rest + 1, 8)
    height = corner + 8 * (up(up(rest, 8) // 8, across) // across)
    cells = [
        (8 * g, min(8, rest - 8 * g), corner + 8 * (g // across), cell * (g % across))
        for g in range(up(rest, 8) // 8)
    ]
    return half, rest, cells, strip, strip + rest, height


def operator_kernel(after, h_hbm, w_hbm, m_hbm, copies_hbm, out_ref, h_ref, w_ref, m_ref, left, right, full, sems):
    size, channels = h_ref.shape
    half, rest, cells, strip, diagonal, _ = packing(size)
    load(
        [
            pltpu.make_async_copy(h_hbm.at[:, 0, :], h_ref, sems.at[0]),
            pltpu.make_async_copy(w_hbm, w_ref, sems.at[1]),
            pltpu.make_async_copy(m_hbm, m_ref, sems.at[2]),
        ]
    )
    h = h_ref[...]
    high, low = split(h * (w_ref[...] * m_ref[...].astype(F32)))
    left[:, 0:channels] = high
    left[:, channels : 2 * channels] = high
    left[:, 2 * channels : 3 * channels] = low
    high, low = split(h)
    right[:, 0:channels] = high
    right[:, channels : 2 * channels] = low
    right[:, 2 * channels : 3 * channels] = high
    full[...] = lax.dot_general(
        left[...], right[...], (((1,), (1,)), ((), ())), preferred_element_type=F32
    )
    first = full[0:half, 0:half]
    second = full[half : 2 * half, half : 2 * half]
    row = lax.broadcasted_iota(jnp.int32, (half, half), 0)
    col = lax.broadcasted_iota(jnp.int32, (half, half), 1)
    out_ref[strip:, :] = jnp.zeros((out_ref.shape[0] - strip, out_ref.shape[1]), F32)
    out_ref[0:half, 0:half] = jnp.where(row <= col, first, second)
    out_ref[0:half, half : 2 * half] = full[0:half, half : 2 * half]
    out_ref[strip : strip + rest, :] = full[2 * half : size, 0 : 2 * half]
    for row_at, take, at, lane in cells:
        out_ref[at : at + take, lane : lane + rest] = full[
            2 * half + row_at : 2 * half + row_at + take, 2 * half : size
        ]
    out_ref[diagonal : diagonal + 1, 0:half] = jnp.sum(
        jnp.where(row == col, second, 0.0), axis=0, keepdims=True
    )
    if len(copies_hbm.shape) == 2:
        load([pltpu.make_async_copy(out_ref, copies_hbm, sems.at[0])])
    else:
        load([pltpu.make_async_copy(out_ref, copies_hbm.at[k], sems.at[k]) for k in range(copies_hbm.shape[0])])


def make_unit(unit, turn):
    row = lax.broadcasted_iota(jnp.int32, unit.shape, 0)
    col = lax.broadcasted_iota(jnp.int32, unit.shape, 1)
    unit[...] = jnp.where(row == col, 1.0, 0.0).astype(BF16)
    turn[...] = jnp.zeros(turn.shape, BF16)


def unpack_kernel(other, size, after, packed_hbm, *refs):
    out_ref, slots, turn, unit, sems = [*refs[other:][:1], *refs[-4:]]
    kind = lax.rem(lax.axis_index("region") + other, 2)
    pairs = slots.shape[0]

    def fetch(k):
        return pltpu.make_async_copy(packed_hbm.at[k], slots.at[k], sems.at[k])

    for k in range(pairs):
        fetch(k).start()
    make_unit(unit, turn)
    for k in range(pairs):
        fetch(k).wait()

    def one_block(k, carry):
        unfold(size, slots.at[k], out_ref.at[2 * k + kind], turn, unit)
        return carry

    lax.fori_loop(0, pairs, one_block, 0)


def unpack_all_kernel(regions, after, packed_hbm, out_hbm, slots, turn, unit, stacks, sems):
    make_unit(unit, turn)

    def fetch(which):
        slot = lax.rem(which, 2)
        return pltpu.make_async_copy(packed_hbm.at[which], slots.at[slot], sems.at[slot])

    def one_owner(owner, carry):
        @pl.when(owner + 1 < regions)
        def _():
            fetch(owner + 1).start()

        fetch(owner).wait()
        unfold(stacks.shape[0], slots.at[lax.rem(owner, 2)], stacks, turn, unit)
        load([pltpu.make_async_copy(stacks, out_hbm.at[owner], sems.at[2])])
        return carry

    fetch(0).start()
    lax.fori_loop(0, regions, one_owner, 0)


def unfold(size, packed_ref, out_ref, turn, unit):
    half, rest, cells, strip, diagonal, _ = packing(size)
    main, over, room = stacking(size)
    gap = up(rest, 16)
    square = split(packed_ref[0:half, 0:half])
    side = split(packed_ref[0:half, half : 2 * half])
    stripe = split(packed_ref[strip : strip + rest, :])
    for k in range(2):
        turn[k * half : (k + 1) * half, :] = square[k]
        turn[(2 + k) * half : (3 + k) * half, :] = side[k]
        for j in range(2):
            at = 4 * half + (2 * k + j) * gap
            turn[at : at + rest, :] = stripe[k][:, j * half : (j + 1) * half]
    turned = lax.dot_general(
        unit[...], turn[...], (((1,), (1,)), ((), ())), preferred_element_type=F32
    )
    row = lax.broadcasted_iota(jnp.int32, (half, half), 0)
    col = lax.broadcasted_iota(jnp.int32, (half, half), 1)
    ends = split(packed_ref[diagonal : diagonal + 1, 0:half])
    if room > over:
        out_ref[:, 3 * main :] = jnp.zeros((size, 3 * room), BF16)

    def put(k, rows, columns, value):
        for at in (0, 1) if k == 0 else (2,):
            if columns < main:
                out_ref[rows : rows + value.shape[0], at * main + columns : at * main + columns + value.shape[1]] = value
            else:
                start = 3 * main + at * room
                out_ref[rows : rows + value.shape[0], start : start + value.shape[1]] = value

    for k in range(2):
        here = square[k].astype(F32)
        there = turned[:, k * half : (k + 1) * half]
        put(k, 0, 0, jnp.where(row <= col, here, there).astype(BF16))
        end = jnp.broadcast_to(ends[k].astype(F32), (half, half))
        put(k, half, half, jnp.where(row > col, here, jnp.where(row == col, end, there)).astype(BF16))
        put(k, 0, half, side[k])
        put(k, half, 0, turned[:, (2 + k) * half : (3 + k) * half].astype(BF16))
        put(k, 2 * half, 0, stripe[k])
        for j in range(2):
            at = 4 * half + (2 * k + j) * gap
            put(k, j * half, 2 * half, turned[:, at : at + rest].astype(BF16))
    for row_at, take, at, lane in cells:
        corner = split(packed_ref[at : at + take, lane : lane + rest])
        for k in range(2):
            put(k, 2 * half + row_at, 2 * half, corner[k])


def first_kernel(depth, s1_hbm, s2_hbm, gain_hbm, m_hbm, pay, back, m_ref, s2, gain, right, sems):
    here = lax.axis_index("tm")
    width = pay.shape[1]

    @pl.when(here == 0)
    def _():
        load([pltpu.make_async_copy(columns_of(s1_hbm, width, 0), pay, sems.at[0])])

    @pl.when(here == depth - 1)
    def _():
        load(
            [
                pltpu.make_async_copy(m_hbm.at[:, 0, :], m_ref, sems.at[0]),
                pltpu.make_async_copy(columns_of(s2_hbm, width, 0), s2, sems.at[1]),
                pltpu.make_async_copy(columns_of(gain_hbm, width, 0), gain, sems.at[2]),
            ]
        )
        stack_left(back, m_ref[...].T)
        stack_right(right, gain[...] * s2[...])
        pay[...] = dot(back[...], right[...])


def rest_kernel(pieces, depth, after, s1_hbm, s2_hbm, gain_hbm, m_hbm, ahead, back, *rest):
    cut, pay = rest[: 3 * pieces], rest[3 * pieces : 4 * pieces - 1]
    m_ref, held, right, sems = rest[4 * pieces - 1 :]
    here = lax.axis_index("tm")
    width = pay[0].shape[1]
    matrix = pltpu.make_async_copy(m_hbm.at[:, 0, :], m_ref, sems.at[0])
    matrix.start()
    reads = [
        pltpu.make_async_copy(columns_of(source, width, i), held.at[k * pieces + i], sems.at[1 + k * pieces + i])
        for k, source in enumerate((s1_hbm, s2_hbm, gain_hbm))
        for i in range(pieces)
    ]
    writes = [
        pltpu.make_async_copy(held.at[n], target, sems.at[1 + 3 * pieces + n])
        for n, target in enumerate(cut)
    ]
    for copy in reads:
        copy.start()
    matrix.wait()
    stack_left(back, m_ref[...].T)
    stack_left(ahead, m_ref[...])
    for read, write in zip(reads, writes):
        read.wait()
        write.start()

    @pl.when(here == 0)
    def _():
        for i in range(1, pieces):
            pay[i - 1][...] = held[i]

    @pl.when(here == depth - 1)
    def _():
        for i in range(1, pieces):
            stack_right(right, held[2 * pieces + i] * held[pieces + i])
            pay[i - 1][...] = dot(back[...], right[...])

    for write in writes:
        write.wait()


def hop_kernel(stage, depth, at, parts, after, behind, s1_ref, s2_ref, gain_ref, in_ref, ahead_ref, back_ref, *rest):
    edge, pays, (keep_ref, right) = rest[: -parts - 2], rest[-parts - 2 : -2], rest[-2:]
    here = lax.axis_index("tm")
    columns = slice(at, at + in_ref.shape[1])
    width = pays[0].shape[1]

    def send(values):
        for k, pay in enumerate(pays):
            pay[...] = values[:, k * width : (k + 1) * width]

    if edge:
        @pl.when((here == 0) | (here == depth - 1))
        def _():
            send(edge[0][:, columns] if edge[0].shape != in_ref.shape else edge[0][...])

    @pl.when(here == stage)
    def _():
        stack_right(right, in_ref[...])
        state = s1_ref[:, columns] + gain_ref[:, columns] * dot(ahead_ref[...], right[...])
        send(state)
        keep_ref[...] = state

    @pl.when(here == depth - 1 - stage)
    def _():
        swept = s2_ref[:, columns] + in_ref[...]
        keep_ref[...] = swept
        stack_right(right, gain_ref[:, columns] * swept)
        send(dot(back_ref[...], right[...]))


def last_kernel(piece, depth, regions, counts, aliased, final, after, behind, owner_ref, ahead_ref, g_ref, s1_ref, s2_ref, gain_ref, *refs):
    groups = []
    for count in counts:
        groups.append(refs[:count])
        refs = refs[count:]
    *kept, inbox = groups
    before, refs = refs[: 2 * aliased], refs[4 * aliased :]
    f_out, g_out, state, total, right, slots, sems = refs
    here = lax.axis_index("tm")
    size, width = total.shape
    resident = slots.shape[0] == 1

    def copy(source, target, which):
        return pltpu.make_async_copy(source, target, sems.at[which])

    def fetch(which):
        slot = lax.rem(which, 2)
        return copy(g_ref.at[which], slots.at[slot], 2 + slot)

    if not resident:
        fetch(0).start()
    writes = [
        copy(source, columns_of(target, width, piece - 1), 4 + k)
        for k, (source, target) in enumerate(zip(before, (f_out, g_out)))
    ]
    for write in writes:
        write.start()

    def lay(target, sources):
        part = width // len(sources)
        for k, source in enumerate(sources):
            target[:, k * part : (k + 1) * part] = source[...]

    @pl.when(here == 0)
    def _():
        lay(total, inbox)
        state[...] = s1_ref[...]
        total[...] += s2_ref[...]

    for stage in range(1, depth - 1):
        @pl.when(here == stage)
        def _():
            lay(state, kept[stage - 1])
            lay(total, kept[depth - 2 - stage])

    @pl.when(here == depth - 1)
    def _():
        lay(total, inbox)
        stack_right(right, total[...])
        state[...] = s1_ref[...] + gain_ref[...] * dot(ahead_ref[...], right[...])
        total[...] = s2_ref[...]

    if final:
        kept_state = copy(state, columns_of(f_out, width, piece), 0)
        kept_state.start()
    stack_right(right, state[...])
    owners = owner_ref[:, piece * width : (piece + 1) * width]

    def one_owner(owner, carry):
        if resident:
            g = g_ref.at[owner]
        else:
            @pl.when(owner + 1 < regions)
            def _():
                fetch(owner + 1).start()

            fetch(owner).wait()
            g = slots.at[lax.rem(owner, 2)]
        seen = dot(g[...], right[...])
        total[...] += jnp.where(owners == owner, seen, 0.0)
        return carry

    lax.fori_loop(0, regions, one_owner, 0)
    if final:
        load([copy(total, columns_of(g_out, width, piece), 1)])
        kept_state.wait()
    for write in writes:
        write.wait()


def body(search_one, search_two, column_gain, model_matrix, obs_owner, observe_matrix, error_weight, channel_mask):
    depth = lax.axis_size("tm")
    regions = lax.axis_size("region")
    size, columns = search_one.shape[1:]
    channels = observe_matrix.shape[3]
    s1, s2, gain = (far(x.reshape(size, 1, columns)) for x in (search_one, search_two, column_gain))
    matrix = far(model_matrix.reshape(size, 1, size))
    observe = far(observe_matrix.reshape(size, 1, channels))
    pieces = 4
    width = columns // pieces
    deep = stacked(size)
    top = depth - 1
    held = pltpu.VMEM((size, width), F32)
    ones = size * width

    def sent(x, *hops):
        return lax.ppermute(x, "tm", list(hops))

    square = pltpu.VMEM((size, deep), BF16)
    pay = [
        pl.pallas_call(
            functools.partial(first_kernel, depth),
            out_shape=held,
            in_specs=[HBM] * 4,
            out_specs=WHOLE,
            scratch_shapes=[
                square,
                pltpu.VMEM((size, size), F32),
                held,
                held,
                pltpu.VMEM((deep, width), BF16),
                pltpu.SemaphoreType.DMA((3,)),
            ],
            compiler_params=params(10),
            cost_estimate=cost(6 * size * ones, 24 * ones),
            name="first",
        )(s1, s2, gain, matrix)
    ]

    def rest_of(after):
        return pl.pallas_call(
            functools.partial(rest_kernel, pieces, depth),
            out_shape=[square] * 2 + ([held] + [pltpu.HBM((size, width), F32)] * (pieces - 1)) * 3 + [held] * (pieces - 1),
            in_specs=[ANY] + [HBM] * 4,
            out_specs=[WHOLE] * 2 + ([WHOLE] + [HBM] * (pieces - 1)) * 3 + [WHOLE] * (pieces - 1),
            scratch_shapes=[
                pltpu.VMEM((size, size), F32),
                pltpu.VMEM((3 * pieces, size, width), F32),
                pltpu.VMEM((deep, width), BF16),
                pltpu.SemaphoreType.DMA((6 * pieces + 1,)),
            ],
            compiler_params=params(16),
            cost_estimate=cost(6 * size * ones, 24 * ones),
            name="rest",
        )(after, s1, s2, gain, matrix)

    half, rows = packing(size)[0], packing(size)[-1]
    resident = regions % 2 == 0 and regions * size * 2 * deep <= 20 * 1024 * 1024
    def own_operator(after):
        return pl.pallas_call(
            operator_kernel,
            out_shape=pltpu.HBM((regions // 2, rows, 2 * half) if resident else (rows, 2 * half), F32),
            in_specs=[ANY] + [HBM] * 3,
            out_specs=HBM,
            scratch_shapes=[
                pltpu.VMEM((rows, 2 * half), F32),
                pltpu.VMEM((size, channels), F32),
                pltpu.VMEM((1, channels), F32),
                pltpu.VMEM((1, channels), jnp.int32),
                pltpu.VMEM((size, 3 * channels), BF16),
                pltpu.VMEM((size, 3 * channels), BF16),
                pltpu.VMEM((size, size), F32),
                pltpu.SemaphoreType.DMA((max(3, regions // 2),)),
            ],
            compiler_params=params(18),
            cost_estimate=cost(6 * size * size * channels, 8 * size * channels),
            name="operator",
        )(after, observe, far(error_weight[0]), far(channel_mask[0]))

    packed = own_operator(pay[0])
    others = rest_of(far(packed))
    ahead, back, *others = others
    s1s, s2s, gains = ([near(x) for x in others[k * pieces : (k + 1) * pieces]] for k in range(3))
    pay = [*pay, *others[3 * pieces :]]
    ahead, back = near(ahead), near(back)
    length = regions // 2
    turn = pltpu.VMEM((4 * half + 4 * up(size - 2 * half, 16), half), BF16)
    unit = pltpu.VMEM((half, half), BF16)
    shape = (regions, size, deep)

    def unpack(after, blocks, before=None):
        other = before is not None
        return pl.pallas_call(
            functools.partial(unpack_kernel, int(other), size),
            out_shape=[pltpu.VMEM(shape, BF16)] + ([] if other else [pltpu.HBM(blocks.shape, F32)]),
            in_specs=[ANY, HBM] + [WHOLE] * other,
            out_specs=[WHOLE] + ([] if other else [HBM]),
            scratch_shapes=[
                pltpu.VMEM((length, rows, 2 * half), F32),
                turn,
                unit,
                pltpu.SemaphoreType.DMA((length,)),
            ],
            input_output_aliases={2: 0} if other else {1: 1},
            compiler_params=params(8),
            cost_estimate=cost(0, size),
            name="unpack",
        )(after, far(blocks), *([near(before)] if other else []))

    def unpack_all(after):
        return pl.pallas_call(
            functools.partial(unpack_all_kernel, regions),
            out_shape=pltpu.HBM(shape, BF16),
            in_specs=[ANY, HBM],
            out_specs=HBM,
            scratch_shapes=[
                pltpu.VMEM((2, rows, 2 * half), F32),
                turn,
                unit,
                pltpu.VMEM(shape[1:], BF16),
                pltpu.SemaphoreType.DMA((3,)),
            ],
            compiler_params=params(24),
            cost_estimate=cost(0, regions * size * size * 8),
            name="unpack",
        )(after, far(gathered))

    def hop(after, behind, stage, i, came, at=0, parts=1, *edge, weight=180):
        taken = came.shape[1]
        shape = (size, taken // parts)
        return pl.pallas_call(
            functools.partial(hop_kernel, stage, depth, at, parts),
            out_shape=[pltpu.VMEM(shape, F32)] * parts + [pltpu.VMEM((size, taken), F32)],
            in_specs=[ANY] * 2 + [WHOLE] * (6 + len(edge)),
            out_specs=[WHOLE] * (parts + 1),
            scratch_shapes=[pltpu.VMEM((deep, taken), BF16)],
            compiler_params=params(8),
            cost_estimate=cost(weight * size * size * taken, 24 * size * taken),
            name="hop",
        )(after, behind, s1s[i], s2s[i], gains[i], near(came), ahead, back, *map(near, edge))

    def last(after, behind, i, done):
        groups = [store[stage, i] for stage in range(1, top)] + [[near(x) for x in inbox[i]]]
        operands = [after, behind, obs_owner, ahead, near(operators) if resident else operators, s1s[i], s2s[i], gains[i], *sum(groups, [])]
        specs = [ANY] * 2 + [WHOLE] * (len(operands) - 2)
        if not resident:
            specs[4] = HBM
        aliases = {}
        if done is not None:
            operands += [near(x) for x in done[2:]]
            aliases = {len(operands): 0, len(operands) + 1: 1}
            operands += list(done[:2])
            specs += [WHOLE] * 2 + [HBM] * 2
        final = i == pieces - 1
        slots = (1, 16, LANES) if resident else (2, size, deep)
        return pl.pallas_call(
            functools.partial(last_kernel, i, depth, regions, [len(g) for g in groups], done is not None, final),
            out_shape=[pltpu.HBM((size, 1, columns), F32)] * 2 + ([] if final else [held] * 2),
            in_specs=specs,
            out_specs=[HBM] * 2 + ([] if final else [WHOLE] * 2),
            scratch_shapes=([held] * 2 if final else [])
            + [
                pltpu.VMEM((deep, width), BF16),
                pltpu.VMEM(slots, BF16),
                pltpu.SemaphoreType.DMA((6,)),
            ],
            input_output_aliases=aliases,
            compiler_params=params(8 if resident else 24),
            cost_estimate=cost(size * ones, size * ones),
            name="last",
        )(*operands)

    def link(low, by=1):
        high = top - low
        return [(low, low + by), (high, high - by)]

    both = link(0) + link(2)
    narrow = width // 2
    store, inbox = {}, {i: [] for i in range(pieces)}

    def keep(stage, i, part):
        store.setdefault((stage, i), []).append(near(part))

    def q(after, i, behind=None):
        out, kept = hop(after, after if behind is None else behind, 1, i, arrived[i])
        keep(1, i, kept)
        return sent(out, *link(1, 1 if i < 2 else 2)), kept

    arrived = [sent(pay[i], *link(0)) for i in range(pieces)]
    middle = [None] * pieces
    if resident:
        kinds = [list(range(kind, regions, 2)) for kind in range(2)]
        alike = lax.all_to_all(packed, "region", 0, 0, axis_index_groups=kinds)
    else:
        gathered = lax.all_gather(packed, "region")

    middle[0], after = q(ahead, 0)
    middle[1], after = q(after, 1)
    out, after = hop(after, after, 2, 0, middle[0])
    keep(2, 0, after)
    inbox[0].append(sent(out, *link(2)))
    middle[2], after = q(after, 2)
    middle[3], after = q(after, 3)
    *outs, after = hop(after, inbox[0][0], 2, 1, middle[1], 0, 2, middle[2])
    keep(2, 1, after)
    turned = [sent(out, *both) for out in outs]
    inbox[1] += turned
    follow = []

    def r2(after, k):
        out, after = hop(after, after, 2, 2, turned[k], k * narrow, 1, middle[3], weight=6)
        keep(2, 2, after)
        follow.append(sent(out, *both))
        return near(after)

    def r3(after, k):
        out, after = hop(after, after, 2, 3, follow[k], k * narrow, weight=6)
        keep(2, 3, after)
        inbox[3].append(sent(out, *link(2)))
        return near(after)

    after = r2(r2(near(after), 0), 1)
    inbox[2] += follow
    if resident:
        operators, alike = unpack(after, alike)
        others = lax.ppermute(far(alike), "region", [(r, r ^ 1) for r in range(regions)])
        operators = near(unpack(after, others, operators)[0])
        after = r3(operators, 0)
    else:
        after = r3(after, 0)
        operators = far(unpack_all(after))
    done = last(after, after, 0, None)
    after = r3(done[3], 1)
    done = last(after, after, 1, done)
    done = last(done[3], inbox[3][0], 2, done)
    done = last(done[3], done[3], 3, done)[:2]
    return tuple(x.reshape(1, size, columns) for x in done)


def solution(mesh):
    return jax.shard_map(
        body,
        mesh=mesh,
        in_specs=(
            P("tm", None, "region"),
            P("tm", None, "region"),
            P("tm", None, "region"),
            P("tm", None, None),
            P("tm", "region"),
            P("tm", "region", None, None),
            P("tm", "region", None),
            P("tm", "region", None),
        ),
        out_specs=(P("tm", None, "region"), P("tm", None, "region")),
        check_vma=False,
    )
```

profile of v0, /device:TPU:14, one launch (start us, length us, event | category | flops | bytes accessed | tf_op | source)
XLA Modules:
  0.0 123.7 jit_solution(14827451604217155766)
XLA Ops:
  0.6 2.8 %first.1.after = f32[548,256]{1,0:T(8,128)S(1)} custom-call(f32[548,1,1024]{2,1,0:T(1,128)} %bitcast.11, f32[548,1,1024]{2,1,0:T(1,128)} %bitcast.13, f32[548,1,1024]{2,1,0:T(1,128)} %bitcast.15, f32[548,1,548]{2,1,0:T(1,128)} %bitcast.17), custom_call_target="tpu_custom_call" | custom-call | flops 461266944 | bytes 3366912 | tf_op jit(solution)/shard_map/first/pallas_call | solution.py:441
  3.4 1.3 %collective-permute-start = (f32[548,256]{1,0:T(8,128)S(1)}, f32[548,256]{1,0:T(8,128)S(1)}, u32[]{:S(2)}, u32[]{:S(2)}) collective-permute-start(f32[548,256]{1,0:T(8,128)S(1)} %first.1.after), channel_id=1, source_target_pairs={{0,8},{24,16},{1,9},{25,17},{2,10},{26,18},{3,11},{27,19},{4,12},{... | collective-permute-start | bytes 1683464 | tf_op jit(solution)/shard_map/ppermute | solution.py:437
  4.7 6.1 %operator.1.after = f32[4,304,512]{2,1,0:T(8,128)} custom-call(f32[548,256]{1,0:T(8,128)S(1)} %first.1.after, f32[548,1,1024]{2,1,0:T(1,128)} %bitcast.19, f32[1,1024]{1,0:T(1,128)} %bitcast.20, s32[1,1024]{1,0:T(1,128)} %bitcast.21), custom_call_target="tpu_custom_call" | custom-call | flops 1845067776 | bytes 4489216 | tf_op jit(solution)/shard_map/operator/pallas_call | solution.py:480
  10.8 5.3 %all-to-all-start = ((f32[4,304,512]{2,1,0:T(8,128)}), f32[4,304,512]{2,1,0:T(8,128)}, u32[]{:S(2)}, u32[]{:S(2)}) async-start(f32[4,304,512]{2,1,0:T(8,128)} %operator.1.after), calls=%async_computation | async-start | bytes 4980736 | tf_op jit(solution)/shard_map/all_to_all | solution.py:613
  16.1 5.6 %rest.1 = (bf16[548,1680]{1,0:T(8,128)(2,1)S(1)}, bf16[548,1680]{1,0:T(8,128)(2,1)S(1)}, f32[548,256]{1,0:T(8,128)S(1)}, f32[548,256]{1,0:T(8,128)}, f32[548,256...) custom-call(f32[4,304,512]{2,1,0:T(8,128)} %operator.1.after, ...), custom_call_target="tpu_custom_call" | custom-call | flops 461266944 | bytes 3366912 | tf_op jit(solution)/shard_map/rest/pallas_call | solution.py:461
  26.7 9.6 %collective-permute-done.1.in_ref = f32[548,256]{1,0:T(8,128)S(1)} collective-permute-done((f32[548,256]{1,0:T(8,128)S(1)}, f32[548,256]{1,0:T(8,128)S(1)}, u32[]{:S(2)}, u32[]{:S(2)}) %collective-permute-start.1) | collective-permute-done | bytes 561184 | tf_op jit(solution)/shard_map/ppermute | solution.py:437
  37.2 1.4 %collective-permute-start.5 = (f32[548,256]{1,0:T(8,128)S(1)}, f32[548,256]{1,0:T(8,128)S(1)}, u32[]{:S(2)}, u32[]{:S(2)}) collective-permute-start(f32[548,256]{1,0:T(8,128)S(1)} %get-tuple-element.79), channel_id=1, source_target_pairs={{16,24},{8,0},{17,25},{9,1},{18,26},{10,2},{19,27},{11,3},{20,28},... | collective-permute-start | bytes 1683464 | tf_op jit(solution)/shard_map/ppermute | solution.py:437
  38.6 9.8 %collective-permute-done.3.in_ref = f32[548,256]{1,0:T(8,128)S(1)} collective-permute-done((f32[548,256]{1,0:T(8,128)S(1)}, f32[548,256]{1,0:T(8,128)S(1)}, u32[]{:S(2)}, u32[]{:S(2)}) %collective-permute-start.3) | collective-permute-done | bytes 561184 | tf_op jit(solution)/shard_map/ppermute | solution.py:437
  48.7 1.4 %collective-permute-start.7 = (f32[548,256]{1,0:T(8,128)S(1)}, f32[548,256]{1,0:T(8,128)S(1)}, u32[]{:S(2)}, u32[]{:S(2)}) collective-permute-start(f32[548,256]{1,0:T(8,128)S(1)} %get-tuple-element.81), channel_id=1, source_target_pairs={{8,24},{16,0},{9,25},{17,1},{10,26},{18,2},{11,27},{19,3},{12,28},... | collective-permute-start | bytes 1683464 | tf_op jit(solution)/shard_map/ppermute | solution.py:437
  50.1 8.9 %collective-permute-done.4.in_ref = f32[548,256]{1,0:T(8,128)S(1)} collective-permute-done((f32[548,256]{1,0:T(8,128)S(1)}, f32[548,256]{1,0:T(8,128)S(1)}, u32[]{:S(2)}, u32[]{:S(2)}) %collective-permute-start.4) | collective-permute-done | bytes 561184 | tf_op jit(solution)/shard_map/ppermute | solution.py:437
  60.4 3.5 %collective-permute-done.5.behind.refs_2_ = f32[548,256]{1,0:T(8,128)S(1)} collective-permute-done((f32[548,256]{1,0:T(8,128)S(1)}, f32[548,256]{1,0:T(8,128)S(1)}, u32[]{:S(2)}, u32[]{:S(2)}) %collective-permute-start.5) | collective-permute-done | bytes 561184 | tf_op jit(solution)/shard_map/ppermute | solution.py:437
  64.7 2.0 %collective-permute-start.10 = (f32[548,128]{1,0:T(8,128)S(1)}, f32[548,128]{1,0:T(8,128)S(1)}, u32[]{:S(2)}, u32[]{:S(2)}) collective-permute-start(f32[548,128]{1,0:T(8,128)S(1)} %get-tuple-element.86), channel_id=1, source_target_pairs={{0,8},{24,16},{16,24},{8,0},{1,9},{25,17},{17,25},{9,1},{2,10},{26... | collective-permute-start | bytes 841736 | tf_op jit(solution)/shard_map/ppermute | solution.py:437
  66.7 8.0 %collective-permute-done.9.rest_0_ = f32[548,256]{1,0:T(8,128)S(1)} collective-permute-done((f32[548,256]{1,0:T(8,128)S(1)}, f32[548,256]{1,0:T(8,128)S(1)}, u32[]{:S(2)}, u32[]{:S(2)}) %collective-permute-start.9) | collective-permute-done | bytes 561184 | tf_op jit(solution)/shard_map/ppermute | solution.py:437
  78.3 3.8 %unpack.2 = (bf16[8,548,1680]{2,1,0:T(8,128)(2,1)S(1)}, f32[4,304,512]{2,1,0:T(8,128)}) custom-call(f32[548,128]{1,0:T(8,128)S(1)} %get-tuple-element.87.after.refs_2_, f32[4,304,512]{2,1,0:T(8,128)} %all-to-all-done.packed_hbm), custom_call_target="tpu_custom_call", output_to_operand_aliasing={{1}: (1, {})} | custom-call | bytes 548 | tf_op jit(solution)/shard_map/unpack/pallas_call | solution.py:513
  82.2 2.5 %collective-permute-start.12 = (f32[548,128]{1,0:T(8,128)S(1)}, f32[548,128]{1,0:T(8,128)S(1)}, u32[]{:S(2)}, u32[]{:S(2)}) collective-permute-start(f32[548,128]{1,0:T(8,128)S(1)} %copy-done.48), channel_id=1, source_target_pairs={{0,8},{24,16},{16,24},{8,0},{1,9},{25,17},{17,25},{9,1},{2,10},{26... | collective-permute-start | bytes 841736 | tf_op jit(solution)/shard_map/ppermute | solution.py:437
  84.8 2.3 %collective-permute-done.11.packed_hbm = f32[4,304,512]{2,1,0:T(8,128)S(1)} collective-permute-done((f32[4,304,512]{2,1,0:T(8,128)}, f32[4,304,512]{2,1,0:T(8,128)S(1)}, u32[]{:S(2)}, u32[]{:S(2)}) %collective-permute-start.11) | collective-permute-done | bytes 2490400 | tf_op jit(solution)/shard_map/ppermute | solution.py:646
  87.1 1.4 %copy-done.49 = f32[4,304,512]{2,1,0:T(8,128)} copy-done((f32[4,304,512]{2,1,0:T(8,128)}, f32[4,304,512]{2,1,0:T(8,128)S(1)}, u32[]{:S(2)}) %copy-start.49) | copy-done | bytes 2490392
  88.6 3.9 %unpack.3.after.behind.g_ref = bf16[8,548,1680]{2,1,0:T(8,128)(2,1)S(1)} custom-call(f32[548,128]{1,0:T(8,128)S(1)} %get-tuple-element.87.after.refs_2_, f32[4,304,512]{2,1,0:T(8,128)} %copy-done.49, bf16[8,548,1680]{2,1,0:T(8,128)(2,1)S(1)} %get-tuple-element.89.refs_0_), custom_call_target="tpu_custom_call", output_to_operand_aliasing={{}: (2, {})} | custom-call | bytes 548 | tf_op jit(solution)/shard_map/unpack/pallas_call | solution.py:513
  92.7 1.6 %collective-permute-start.14 = (f32[548,128]{1,0:T(8,128)S(1)}, f32[548,128]{1,0:T(8,128)S(1)}, u32[]{:S(2)}, u32[]{:S(2)}) collective-permute-start(f32[548,128]{1,0:T(8,128)S(1)} %get-tuple-element.99), channel_id=1, source_target_pairs={{16,24},{8,0},{17,25},{9,1},{18,26},{10,2},{19,27},{11,3},{20,28},... | collective-permute-start | bytes 841736 | tf_op jit(solution)/shard_map/ppermute | solution.py:437
  94.4 6.5 %last.4 = (f32[548,1,1024]{2,1,0:T(1,128)}, f32[548,1,1024]{2,1,0:T(1,128)}, f32[548,256]{1,0:T(8,128)S(1)}, f32[548,256]{1,0:T(8,128)S(1)}) custom-call(f32[548,128]{1,0:T(8,128)S(1)} %get-tuple-element.91.after.behind.refs_1_, f32[548,128]{1,0:T(8,128)S(1)} %get-tuple-element.91.after.behind.refs_1_, s32[1,1024]{1,0:T(1,128)S(1)} %copy-done.44, ...), custom_call_target="tpu_custom_call" | custom-call | flops 76877824 | bytes 76877824 | tf_op jit(solution)/shard_map/last/pallas_call | solution.py:576
  101.0 1.6 %collective-permute-start.15 = (f32[548,128]{1,0:T(8,128)S(1)}, f32[548,128]{1,0:T(8,128)S(1)}, u32[]{:S(2)}, u32[]{:S(2)}) collective-permute-start(f32[548,128]{1,0:T(8,128)S(1)} %get-tuple-element.104), channel_id=1, source_target_pairs={{16,24},{8,0},{17,25},{9,1},{18,26},{10,2},{19,27},{11,3},{20,28},... | collective-permute-start | bytes 841736 | tf_op jit(solution)/shard_map/ppermute | solution.py:437
  102.8 6.7 %last.5 = (f32[548,1,1024]{2,1,0:T(1,128)}, f32[548,1,1024]{2,1,0:T(1,128)}, f32[548,256]{1,0:T(8,128)S(1)}, f32[548,256]{1,0:T(8,128)S(1)}) custom-call(f32[548,128]{1,0:T(8,128)S(1)} %get-tuple-element.94.after.behind.refs_2_, f32[548,128]{1,0:T(8,128)S(1)} %get-tuple-element.94.after.behind.refs_2_, ...), custom_call_target="tpu_custom_call", output_to_operand_aliasing={{0}: (14, {}), {1}: (15, {})} | custom-call | flops 76877824 | bytes 76877824 | tf_op jit(solution)/shard_map/last/pallas_call | solution.py:576
  109.6 6.5 %last.6 = (f32[548,1,1024]{2,1,0:T(1,128)}, f32[548,1,1024]{2,1,0:T(1,128)}, f32[548,256]{1,0:T(8,128)S(1)}, f32[548,256]{1,0:T(8,128)S(1)}) custom-call(f32[548,256]{1,0:T(8,128)S(1)} %get-tuple-element.98.after.refs_6_, f32[548,128]{1,0:T(8,128)S(1)} %collective-permute-done.14.behind.refs_3_, ...), custom_call_target="tpu_custom_call", output_to_operand_aliasing={{0}: (15, {}), {1}: (16, {})} | custom-call | flops 76877824 | bytes 76877824 | tf_op jit(solution)/shard_map/last/pallas_call | solution.py:576
  116.2 7.3 %last.7 = (f32[548,1,1024]{2,1,0:T(1,128)}, f32[548,1,1024]{2,1,0:T(1,128)}) custom-call(f32[548,256]{1,0:T(8,128)S(1)} %get-tuple-element.103.after.behind.refs_6_, f32[548,256]{1,0:T(8,128)S(1)} %get-tuple-element.103.after.behind.refs_6_, s32[1,1024]{1,0:T(1,128)S(1)} %copy-done.44, ...), custom_call_target="tpu_custom_call", output_to_operand_aliasing={{0}: (15, {}), {1}: (16, {})} | custom-call | flops 76877824 | bytes 76877824 | tf_op jit(solution)/shard_map/last/pallas_call | solution.py:576
  (129 shorter events, 12.2 us)
Async XLA Ops:
  3.4 22.4 %collective-permute-start = (f32[548,256]{1,0:T(8,128)S(1)}, f32[548,256]{1,0:T(8,128)S(1)}, u32[]{:S(2)}, u32[]{:S(2)}) collective-permute-start(f32[548,256]{1,0:T(8,128)S(1)} %first.1.after), channel_id=1, source_target_pairs={{0,8},{24,16},{1,9},{25,17},{2,10},{26,18},{3,11},{27,19},{4,12},{... | collective-permute-start | bytes 1683464 | tf_op jit(solution)/shard_map/ppermute | solution.py:437
  10.8 67.5 %all-to-all-start = ((f32[4,304,512]{2,1,0:T(8,128)}), f32[4,304,512]{2,1,0:T(8,128)}, u32[]{:S(2)}, u32[]{:S(2)}) async-start(f32[4,304,512]{2,1,0:T(8,128)} %operator.1.after), calls=%async_computation | async-start | bytes 4980736 | tf_op jit(solution)/shard_map/all_to_all | solution.py:613
  21.7 15.3 %copy-start.20 = (f32[548,256]{1,0:T(8,128)}, f32[548,256]{1,0:T(8,128)S(1)}, u32[]{:S(2)}) copy-start(f32[548,256]{1,0:T(8,128)S(1)} %get-tuple-element.57.s1_ref) | copy-start | bytes 1683460
  21.7 15.3 %copy-start.22 = (f32[548,256]{1,0:T(8,128)}, f32[548,256]{1,0:T(8,128)S(1)}, u32[]{:S(2)}) copy-start(f32[548,256]{1,0:T(8,128)S(1)} %get-tuple-element.58.s2_ref) | copy-start | bytes 1683460
  21.8 15.3 %copy-start.24 = (f32[548,256]{1,0:T(8,128)}, f32[548,256]{1,0:T(8,128)S(1)}, u32[]{:S(2)}) copy-start(f32[548,256]{1,0:T(8,128)S(1)} %get-tuple-element.59.gain_ref) | copy-start | bytes 1683460
  21.8 54.4 %copy-start = (bf16[548,1680]{1,0:T(8,128)(2,1)}, bf16[548,1680]{1,0:T(8,128)(2,1)S(1)}, u32[]{:S(2)}) copy-start(bf16[548,1680]{1,0:T(8,128)(2,1)S(1)} %get-tuple-element.60.back_ref) | copy-start | bytes 5523844
  21.8 14.5 %collective-permute-start.1 = (f32[548,256]{1,0:T(8,128)S(1)}, f32[548,256]{1,0:T(8,128)S(1)}, u32[]{:S(2)}, u32[]{:S(2)}) collective-permute-start(f32[548,256]{1,0:T(8,128)S(1)} %get-tuple-element.65), channel_id=1, source_target_pairs={{0,8},{24,16},{1,9},{25,17},{2,10},{26,18},{3,11},{27,19},{4,12},{... | collective-permute-start | bytes 1683464 | tf_op jit(solution)/shard_map/ppermute | solution.py:437
  23.1 25.3 %collective-permute-start.3 = (f32[548,256]{1,0:T(8,128)S(1)}, f32[548,256]{1,0:T(8,128)S(1)}, u32[]{:S(2)}, u32[]{:S(2)}) collective-permute-start(f32[548,256]{1,0:T(8,128)S(1)} %get-tuple-element.72), channel_id=1, source_target_pairs={{0,8},{24,16},{1,9},{25,17},{2,10},{26,18},{3,11},{27,19},{4,12},{... | collective-permute-start | bytes 1683464 | tf_op jit(solution)/shard_map/ppermute | solution.py:437
  24.4 34.6 %collective-permute-start.4 = (f32[548,256]{1,0:T(8,128)S(1)}, f32[548,256]{1,0:T(8,128)S(1)}, u32[]{:S(2)}, u32[]{:S(2)}) collective-permute-start(f32[548,256]{1,0:T(8,128)S(1)} %get-tuple-element.77), channel_id=1, source_target_pairs={{0,8},{24,16},{1,9},{25,17},{2,10},{26,18},{3,11},{27,19},{4,12},{... | collective-permute-start | bytes 1683464 | tf_op jit(solution)/shard_map/ppermute | solution.py:437
  25.9 11.2 %collective-permute-start.2 = (f32[548,256]{1,0:T(8,128)S(1)}, f32[548,256]{1,0:T(8,128)S(1)}, u32[]{:S(2)}, u32[]{:S(2)}) collective-permute-start(f32[548,256]{1,0:T(8,128)S(1)} %get-tuple-element.67), channel_id=1, source_target_pairs={{8,16},{16,8},{9,17},{17,9},{10,18},{18,10},{11,19},{19,11},{12,20... | collective-permute-start | bytes 1683464 | tf_op jit(solution)/shard_map/ppermute | solution.py:437
  36.3 24.1 %collective-permute-start.6 = (f32[548,256]{1,0:T(8,128)S(1)}, f32[548,256]{1,0:T(8,128)S(1)}, u32[]{:S(2)}, u32[]{:S(2)}) collective-permute-start(f32[548,256]{1,0:T(8,128)S(1)} %get-tuple-element.80), channel_id=1, source_target_pairs={{8,16},{16,8},{9,17},{17,9},{10,18},{18,10},{11,19},{19,11},{12,20... | collective-permute-start | bytes 1683464 | tf_op jit(solution)/shard_map/ppermute | solution.py:437
  37.1 11.3 %copy-start.2 = (f32[548,256]{1,0:T(8,128)S(1)}, f32[548,256]{1,0:T(8,128)}, u32[]{:S(2)}) copy-start(f32[548,256]{1,0:T(8,128)} %get-tuple-element.69.s1_ref) | copy-start | bytes 1683460
  37.1 11.3 %copy-start.3 = (f32[548,256]{1,0:T(8,128)S(1)}, f32[548,256]{1,0:T(8,128)}, u32[]{:S(2)}) copy-start(f32[548,256]{1,0:T(8,128)} %get-tuple-element.70.s2_ref) | copy-start | bytes 1683460
  37.2 11.5 %copy-start.28 = (f32[548,256]{1,0:T(8,128)}, f32[548,256]{1,0:T(8,128)S(1)}, u32[]{:S(2)}) copy-start(f32[548,256]{1,0:T(8,128)S(1)} %get-tuple-element.68.after.behind.refs_1_) | copy-start | bytes 1683460
  37.2 26.7 %collective-permute-start.5 = (f32[548,256]{1,0:T(8,128)S(1)}, f32[548,256]{1,0:T(8,128)S(1)}, u32[]{:S(2)}, u32[]{:S(2)}) collective-permute-start(f32[548,256]{1,0:T(8,128)S(1)} %get-tuple-element.79), channel_id=1, source_target_pairs={{16,24},{8,0},{17,25},{9,1},{18,26},{10,2},{19,27},{11,3},{20,28},... | collective-permute-start | bytes 1683464 | tf_op jit(solution)/shard_map/ppermute | solution.py:437
  48.7 15.2 %collective-permute-start.7 = (f32[548,256]{1,0:T(8,128)S(1)}, f32[548,256]{1,0:T(8,128)S(1)}, u32[]{:S(2)}, u32[]{:S(2)}) collective-permute-start(f32[548,256]{1,0:T(8,128)S(1)} %get-tuple-element.81), channel_id=1, source_target_pairs={{8,24},{16,0},{9,25},{17,1},{10,26},{18,2},{11,27},{19,3},{12,28},... | collective-permute-start | bytes 1683464 | tf_op jit(solution)/shard_map/ppermute | solution.py:437
  59.1 15.6 %collective-permute-start.9 = (f32[548,256]{1,0:T(8,128)S(1)}, f32[548,256]{1,0:T(8,128)S(1)}, u32[]{:S(2)}, u32[]{:S(2)}) collective-permute-start(f32[548,256]{1,0:T(8,128)S(1)} %get-tuple-element.84), channel_id=1, source_target_pairs={{8,24},{16,0},{9,25},{17,1},{10,26},{18,2},{11,27},{19,3},{12,28},... | collective-permute-start | bytes 1683464 | tf_op jit(solution)/shard_map/ppermute | solution.py:437
  64.7 10.0 %collective-permute-start.8 = (f32[548,128]{1,0:T(8,128)S(1)}, f32[548,128]{1,0:T(8,128)S(1)}, u32[]{:S(2)}, u32[]{:S(2)}) collective-permute-start(f32[548,128]{1,0:T(8,128)S(1)} %get-tuple-element.83), channel_id=1, source_target_pairs={{0,8},{24,16},{16,24},{8,0},{1,9},{25,17},{17,25},{9,1},{2,10},{26... | collective-permute-start | bytes 841736 | tf_op jit(solution)/shard_map/ppermute | solution.py:437
  64.7 11.5 %collective-permute-start.10 = (f32[548,128]{1,0:T(8,128)S(1)}, f32[548,128]{1,0:T(8,128)S(1)}, u32[]{:S(2)}, u32[]{:S(2)}) collective-permute-start(f32[548,128]{1,0:T(8,128)S(1)} %get-tuple-element.86), channel_id=1, source_target_pairs={{0,8},{24,16},{16,24},{8,0},{1,9},{25,17},{17,25},{9,1},{2,10},{26... | collective-permute-start | bytes 841736 | tf_op jit(solution)/shard_map/ppermute | solution.py:437
  82.1 5.0 %collective-permute-start.11 = (f32[4,304,512]{2,1,0:T(8,128)}, f32[4,304,512]{2,1,0:T(8,128)S(1)}, u32[]{:S(2)}, u32[]{:S(2)}) collective-permute-start(f32[4,304,512]{2,1,0:T(8,128)} %get-tuple-element.88), channel_id=1, source_target_pairs={{0,1},{1,0},{2,3},{3,2},{4,5},{5,4},{6,7},{7,6},{8,9},{9,8},{10,11... | collective-permute-start | bytes 7471112 | tf_op jit(solution)/shard_map/ppermute | solution.py:646
  82.2 10.4 %collective-permute-start.12 = (f32[548,128]{1,0:T(8,128)S(1)}, f32[548,128]{1,0:T(8,128)S(1)}, u32[]{:S(2)}, u32[]{:S(2)}) collective-permute-start(f32[548,128]{1,0:T(8,128)S(1)} %copy-done.48), channel_id=1, source_target_pairs={{0,8},{24,16},{16,24},{8,0},{1,9},{25,17},{17,25},{9,1},{2,10},{26... | collective-permute-start | bytes 841736 | tf_op jit(solution)/shard_map/ppermute | solution.py:437
  84.7 16.2 %collective-permute-start.13 = (f32[548,128]{1,0:T(8,128)S(1)}, f32[548,128]{1,0:T(8,128)S(1)}, u32[]{:S(2)}, u32[]{:S(2)}) collective-permute-start(f32[548,128]{1,0:T(8,128)S(1)} %copy-done.46), channel_id=1, source_target_pairs={{0,8},{24,16},{16,24},{8,0},{1,9},{25,17},{17,25},{9,1},{2,10},{26... | collective-permute-start | bytes 841736 | tf_op jit(solution)/shard_map/ppermute | solution.py:437
  92.7 16.9 %collective-permute-start.14 = (f32[548,128]{1,0:T(8,128)S(1)}, f32[548,128]{1,0:T(8,128)S(1)}, u32[]{:S(2)}, u32[]{:S(2)}) collective-permute-start(f32[548,128]{1,0:T(8,128)S(1)} %get-tuple-element.99), channel_id=1, source_target_pairs={{16,24},{8,0},{17,25},{9,1},{18,26},{10,2},{19,27},{11,3},{20,28},... | collective-permute-start | bytes 841736 | tf_op jit(solution)/shard_map/ppermute | solution.py:437
  101.0 15.1 %collective-permute-start.15 = (f32[548,128]{1,0:T(8,128)S(1)}, f32[548,128]{1,0:T(8,128)S(1)}, u32[]{:S(2)}, u32[]{:S(2)}) collective-permute-start(f32[548,128]{1,0:T(8,128)S(1)} %get-tuple-element.104), channel_id=1, source_target_pairs={{16,24},{8,0},{17,25},{9,1},{18,26},{10,2},{19,27},{11,3},{20,28},... | collective-permute-start | bytes 841736 | tf_op jit(solution)/shard_map/ppermute | solution.py:437
  (43 other events, 194.6 us)
where the time goes:
time: 126 us; the launch traced here: 124 us
  Pallas kernels  49.6 us (39%)
  waiting for transfers between devices  42.2 us (33%)
  starting transfers between devices  24.1 us (19%)
  local copies, waits for them, and re-layouts  6.21 us (5%)
  between operations  1.59 us (1%)
    ppermute x15, waiting for transfers between devices, sent(): return lax.ppermute(x, 'tm', list(hops))  39.9 us
    pallas_call x4, Pallas kernels, last(): pl.pallas_call(functools.partial(last_kernel, i, depth, regions, [len(g)...  27.1 us
    ppermute x15, starting transfers between devices, sent(): return lax.ppermute(x, 'tm', list(hops))  18.7 us
    pallas_call x2, Pallas kernels, unpack(): pl.pallas_call(functools.partial(unpack_kernel, int(other), size), out_sh...  7.73 us
    unnamed x100, local copies, waits for them, and re-layouts  6.21 us
    pallas_call x1, Pallas kernels, own_operator(): pl.pallas_call(operator_kernel, out_shape=pltpu.HBM((regions // 2, rows,...  6.08 us
    pallas_call x1, Pallas kernels, rest_of(): pl.pallas_call(functools.partial(rest_kernel, pieces, depth), out_shape=[...  5.58 us
    all_to_all x1, starting transfers between devices, body(): alike = lax.all_to_all(packed, 'region', 0, 0, axis_index_groups=kinds)  5.33 us
  transfers between devices with their start and end apart: 17, of which 6 were waited for; matrix products, arithmetic and copies ran while one was open for 0% of the time, Pallas kernels for 29%

commit v1 on v0

--- a/solution.py
+++ b/solution.py
@@ -156,25 +156,28 @@
     turn[...] = jnp.zeros(turn.shape, BF16)
 
 
-def unpack_kernel(other, size, after, packed_hbm, *refs):
-    out_ref, slots, turn, unit, sems = [*refs[other:][:1], *refs[-4:]]
+def unpack_kernel(other, size, after, *refs):
+    slots, turn, unit, sems = refs[-4:]
+    pairs = slots.shape[0]
+    blocks, out_ref = (refs[:pairs], refs[pairs + 1]) if other else ([refs[0].at[k] for k in range(pairs)], refs[1])
     kind = lax.rem(lax.axis_index("region") + other, 2)
-    pairs = slots.shape[0]
-
-    def fetch(k):
-        return pltpu.make_async_copy(packed_hbm.at[k], slots.at[k], sems.at[k])
-
-    for k in range(pairs):
-        fetch(k).start()
+    fetches = [pltpu.make_async_copy(blocks[k], slots.at[k], sems.at[k]) for k in range(pairs)]
+    passes = [pltpu.make_async_copy(slots.at[k], refs[2 + k], sems.at[pairs + k]) for k in range(pairs * (1 - other))]
+    for fetch in fetches:
+        fetch.start()
     make_unit(unit, turn)
-    for k in range(pairs):
-        fetch(k).wait()
+    for fetch in fetches:
+        fetch.wait()
+    for passing in passes:
+        passing.start()
 
     def one_block(k, carry):
         unfold(size, slots.at[k], out_ref.at[2 * k + kind], turn, unit)
         return carry
 
     lax.fori_loop(0, pairs, one_block, 0)
+    for passing in passes:
+        passing.wait()
 
 
 def unpack_all_kernel(regions, after, packed_hbm, out_hbm, slots, turn, unit, stacks, sems):
@@ -318,9 +321,10 @@
         for k, pay in enumerate(pays):
             pay[...] = values[:, k * width : (k + 1) * width]
 
-    if edge:
-        @pl.when((here == 0) | (here == depth - 1))
-        def _():
+    @pl.when((here == 0) | (here == depth - 1))
+    def _():
+        keep_ref[...] = in_ref[...]
+        if edge:
             send(edge[0][:, columns] if edge[0].shape != in_ref.shape else edge[0][...])
 
     @pl.when(here == stage)
@@ -512,20 +516,20 @@
         other = before is not None
         return pl.pallas_call(
             functools.partial(unpack_kernel, int(other), size),
-            out_shape=[pltpu.VMEM(shape, BF16)] + ([] if other else [pltpu.HBM(blocks.shape, F32)]),
-            in_specs=[ANY, HBM] + [WHOLE] * other,
-            out_specs=[WHOLE] + ([] if other else [HBM]),
+            out_shape=[pltpu.VMEM(shape, BF16)] + [pltpu.HBM((rows, 2 * half), F32)] * (length * (not other)),
+            in_specs=[ANY] + [HBM] * len(blocks) + [WHOLE] * other,
+            out_specs=[WHOLE] + [HBM] * (length * (not other)),
             scratch_shapes=[
                 pltpu.VMEM((length, rows, 2 * half), F32),
                 turn,
                 unit,
-                pltpu.SemaphoreType.DMA((length,)),
+                pltpu.SemaphoreType.DMA((2 * length,)),
             ],
-            input_output_aliases={2: 0} if other else {1: 1},
+            input_output_aliases={1 + len(blocks): 0} if other else {},
             compiler_params=params(8),
             cost_estimate=cost(0, size),
             name="unpack",
-        )(after, far(blocks), *([near(before)] if other else []))
+        )(after, *map(far, blocks), *([near(before)] if other else []))
 
     def unpack_all(after):
         return pl.pallas_call(
@@ -624,11 +628,10 @@
     *outs, after = hop(after, inbox[0][0], 2, 1, middle[1], 0, 2, middle[2])
     keep(2, 1, after)
     turned = [sent(out, *both) for out in outs]
-    inbox[1] += turned
     follow = []
 
     def r2(after, k):
-        out, after = hop(after, after, 2, 2, turned[k], k * narrow, 1, middle[3], weight=6)
+        out, after = hop(after, after, 2, 2, turned[k], k * narrow, 1, middle[3])
         keep(2, 2, after)
         follow.append(sent(out, *both))
         return near(after)
@@ -639,19 +642,20 @@
         inbox[3].append(sent(out, *link(2)))
         return near(after)
 
-    after = r2(r2(near(after), 0), 1)
-    inbox[2] += follow
     if resident:
-        operators, alike = unpack(after, alike)
-        others = lax.ppermute(far(alike), "region", [(r, r ^ 1) for r in range(regions)])
+        operators, *alike = unpack(near(after), [alike])
+        others = [lax.ppermute(far(x), "region", [(r, r ^ 1) for r in range(regions)]) for x in alike]
+        after = r2(r2(near(operators), 0), 1)
         operators = near(unpack(after, others, operators)[0])
         after = r3(operators, 0)
     else:
-        after = r3(after, 0)
+        after = r3(r2(r2(after, 0), 1), 0)
         operators = far(unpack_all(after))
+    inbox[1] = store[2, 2]
     done = last(after, after, 0, None)
     after = r3(done[3], 1)
     done = last(after, after, 1, done)
+    inbox[2] = store[2, 3]
     done = last(done[3], inbox[3][0], 2, done)
     done = last(done[3], done[3], 3, done)[:2]
     return tuple(x.reshape(1, size, columns) for x in done)

time: 126 us -> 123 us (0.976); the launches traced: 124 us -> 122 us
  waiting for transfers between devices: 42.2 us -> 35.3 us
  Pallas kernels: 49.6 us -> 54 us
  starting transfers between devices: 24.1 us -> 25.8 us
    ppermute x15, waiting for transfers between devices: 39.9 us -> 31.9 us  [sent(): return lax.ppermute(x, 'tm', list(hops))]
    pallas_call x10, Pallas kernels: 0.39 us -> 4.82 us  [hop(): pl.pallas_call(functools.partial(hop_kernel, stage, depth, at, parts), ou...]
    all_to_all x1, waiting for transfers between devices: 0.01 us -> 1.77 us  [body(): alike = lax.all_to_all(packed, 'region', 0, 0, axis_index_groups=kinds)]
    unnamed x100 -> x98, local copies, waits for them, and re-layouts: 6.21 us -> 5.29 us
  transfers between devices with their start and end apart: 17 -> 20, of which waited for: 6 -> 9; matrix products, arithmetic and copies ran while one was open for 0% -> 0% of each run, Pallas kernels for 29% -> 36%
where the time goes in v1:
time: 123 us; the launch traced here: 122 us
  Pallas kernels  54 us (44%)
  waiting for transfers between devices  35.3 us (29%)
  starting transfers between devices  25.8 us (21%)
  local copies, waits for them, and re-layouts  5.29 us (4%)
  between operations  1.53 us (1%)
    ppermute x15, waiting for transfers between devices, sent(): return lax.ppermute(x, 'tm', list(hops))  31.9 us
    pallas_call x4, Pallas kernels, last(): pl.pallas_call(functools.partial(last_kernel, i, depth, regions, [len(g)...  27.1 us
    ppermute x15, starting transfers between devices, sent(): return lax.ppermute(x, 'tm', list(hops))  19.5 us
    pallas_call x2, Pallas kernels, unpack(): pl.pallas_call(functools.partial(unpack_kernel, int(other), size), out_sh...  7.72 us
    pallas_call x1, Pallas kernels, own_operator(): pl.pallas_call(operator_kernel, out_shape=pltpu.HBM((regions // 2, rows,...  6.09 us
    pallas_call x1, Pallas kernels, rest_of(): pl.pallas_call(functools.partial(rest_kernel, pieces, depth), out_shape=[...  5.58 us
    all_to_all x1, starting transfers between devices, body(): alike = lax.all_to_all(packed, 'region', 0, 0, axis_index_groups=kinds)  5.33 us
    unnamed x98, local copies, waits for them, and re-layouts  5.29 us
  transfers between devices with their start and end apart: 20, of which 9 were waited for; matrix products, arithmetic and copies ran while one was open for 0% of the time, Pallas kernels for 36%

profile of v1, /device:TPU:14, one launch (start us, length us, event | category | flops | bytes accessed | tf_op | source)
XLA Modules:
  0.0 122.0 jit_solution(18026169593625885081)
XLA Ops:
  0.6 2.8 %first.1.after = f32[548,256]{1,0:T(8,128)S(1)} custom-call(f32[548,1,1024]{2,1,0:T(1,128)} %bitcast.11, f32[548,1,1024]{2,1,0:T(1,128)} %bitcast.13, f32[548,1,1024]{2,1,0:T(1,128)} %bitcast.15, f32[548,1,548]{2,1,0:T(1,128)} %bitcast.17), custom_call_target="tpu_custom_call" | custom-call | flops 461266944 | bytes 3366912 | tf_op jit(solution)/shard_map/first/pallas_call | solution.py:445
  3.4 1.3 %collective-permute-start = (f32[548,256]{1,0:T(8,128)S(1)}, f32[548,256]{1,0:T(8,128)S(1)}, u32[]{:S(2)}, u32[]{:S(2)}) collective-permute-start(f32[548,256]{1,0:T(8,128)S(1)} %first.1.after), channel_id=1, source_target_pairs={{0,8},{24,16},{1,9},{25,17},{2,10},{26,18},{3,11},{27,19},{4,12},{... | collective-permute-start | bytes 1683464 | tf_op jit(solution)/shard_map/ppermute | solution.py:441
  4.7 6.1 %operator.1.after = f32[4,304,512]{2,1,0:T(8,128)} custom-call(f32[548,256]{1,0:T(8,128)S(1)} %first.1.after, f32[548,1,1024]{2,1,0:T(1,128)} %bitcast.19, f32[1,1024]{1,0:T(1,128)} %bitcast.20, s32[1,1024]{1,0:T(1,128)} %bitcast.21), custom_call_target="tpu_custom_call" | custom-call | flops 1845067776 | bytes 4489216 | tf_op jit(solution)/shard_map/operator/pallas_call | solution.py:484
  10.8 5.3 %all-to-all-start = ((f32[4,304,512]{2,1,0:T(8,128)}), f32[4,304,512]{2,1,0:T(8,128)}, u32[]{:S(2)}, u32[]{:S(2)}) async-start(f32[4,304,512]{2,1,0:T(8,128)} %operator.1.after), calls=%async_computation | async-start | bytes 4980736 | tf_op jit(solution)/shard_map/all_to_all | solution.py:617
  16.2 5.6 %rest.1 = (bf16[548,1680]{1,0:T(8,128)(2,1)S(1)}, bf16[548,1680]{1,0:T(8,128)(2,1)S(1)}, f32[548,256]{1,0:T(8,128)S(1)}, f32[548,256]{1,0:T(8,128)}, f32[548,256...) custom-call(f32[4,304,512]{2,1,0:T(8,128)} %operator.1.after, ...), custom_call_target="tpu_custom_call" | custom-call | flops 461266944 | bytes 3366912 | tf_op jit(solution)/shard_map/rest/pallas_call | solution.py:465
  21.8 1.3 %collective-permute-start.1 = (f32[548,256]{1,0:T(8,128)S(1)}, f32[548,256]{1,0:T(8,128)S(1)}, u32[]{:S(2)}, u32[]{:S(2)}) collective-permute-start(f32[548,256]{1,0:T(8,128)S(1)} %get-tuple-element.68), channel_id=1, source_target_pairs={{0,8},{24,16},{1,9},{25,17},{2,10},{26,18},{3,11},{27,19},{4,12},{... | collective-permute-start | bytes 1683464 | tf_op jit(solution)/shard_map/ppermute | solution.py:441
  23.1 1.3 %collective-permute-start.3 = (f32[548,256]{1,0:T(8,128)S(1)}, f32[548,256]{1,0:T(8,128)S(1)}, u32[]{:S(2)}, u32[]{:S(2)}) collective-permute-start(f32[548,256]{1,0:T(8,128)S(1)} %get-tuple-element.75), channel_id=1, source_target_pairs={{0,8},{24,16},{1,9},{25,17},{2,10},{26,18},{3,11},{27,19},{4,12},{... | collective-permute-start | bytes 1683464 | tf_op jit(solution)/shard_map/ppermute | solution.py:441
  26.7 9.6 %collective-permute-done.1.in_ref = f32[548,256]{1,0:T(8,128)S(1)} collective-permute-done((f32[548,256]{1,0:T(8,128)S(1)}, f32[548,256]{1,0:T(8,128)S(1)}, u32[]{:S(2)}, u32[]{:S(2)}) %collective-permute-start.1) | collective-permute-done | bytes 561184 | tf_op jit(solution)/shard_map/ppermute | solution.py:441
  37.3 1.4 %collective-permute-start.5 = (f32[548,256]{1,0:T(8,128)S(1)}, f32[548,256]{1,0:T(8,128)S(1)}, u32[]{:S(2)}, u32[]{:S(2)}) collective-permute-start(f32[548,256]{1,0:T(8,128)S(1)} %get-tuple-element.82), channel_id=1, source_target_pairs={{16,24},{8,0},{17,25},{9,1},{18,26},{10,2},{19,27},{11,3},{20,28},... | collective-permute-start | bytes 1683464 | tf_op jit(solution)/shard_map/ppermute | solution.py:441
  38.7 9.7 %collective-permute-done.3.in_ref = f32[548,256]{1,0:T(8,128)S(1)} collective-permute-done((f32[548,256]{1,0:T(8,128)S(1)}, f32[548,256]{1,0:T(8,128)S(1)}, u32[]{:S(2)}, u32[]{:S(2)}) %collective-permute-start.3) | collective-permute-done | bytes 561184 | tf_op jit(solution)/shard_map/ppermute | solution.py:441
  48.7 1.4 %collective-permute-start.7 = (f32[548,256]{1,0:T(8,128)S(1)}, f32[548,256]{1,0:T(8,128)S(1)}, u32[]{:S(2)}, u32[]{:S(2)}) collective-permute-start(f32[548,256]{1,0:T(8,128)S(1)} %get-tuple-element.84), channel_id=1, source_target_pairs={{8,24},{16,0},{9,25},{17,1},{10,26},{18,2},{11,27},{19,3},{12,28},... | collective-permute-start | bytes 1683464 | tf_op jit(solution)/shard_map/ppermute | solution.py:441
  50.2 8.9 %collective-permute-done.4.in_ref = f32[548,256]{1,0:T(8,128)S(1)} collective-permute-done((f32[548,256]{1,0:T(8,128)S(1)}, f32[548,256]{1,0:T(8,128)S(1)}, u32[]{:S(2)}, u32[]{:S(2)}) %collective-permute-start.4) | collective-permute-done | bytes 561184 | tf_op jit(solution)/shard_map/ppermute | solution.py:441
  61.3 2.6 %collective-permute-done.5.behind.refs_2_ = f32[548,256]{1,0:T(8,128)S(1)} collective-permute-done((f32[548,256]{1,0:T(8,128)S(1)}, f32[548,256]{1,0:T(8,128)S(1)}, u32[]{:S(2)}, u32[]{:S(2)}) %collective-permute-start.5) | collective-permute-done | bytes 561184 | tf_op jit(solution)/shard_map/ppermute | solution.py:441
  65.7 2.0 %collective-permute-start.8 = (f32[548,128]{1,0:T(8,128)}, f32[548,128]{1,0:T(8,128)S(1)}, u32[]{:S(2)}, u32[]{:S(2)}) collective-permute-start(f32[548,128]{1,0:T(8,128)} %get-tuple-element.87), channel_id=1, source_target_pairs={{0,8},{24,16},{16,24},{8,0},{1,9},{25,17},{17,25},{9,1},{2,10},{26... | collective-permute-start | bytes 841736 | tf_op jit(solution)/shard_map/ppermute | solution.py:441
  67.7 1.8 %all-to-all-done.refs_0_ = f32[4,304,512]{2,1,0:T(8,128)} async-done(((f32[4,304,512]{2,1,0:T(8,128)}), f32[4,304,512]{2,1,0:T(8,128)}, u32[]{:S(2)}, u32[]{:S(2)}) %all-to-all-start) | async-done | bytes 2490400 | tf_op jit(solution)/shard_map/all_to_all | solution.py:617
  70.7 3.9 %unpack.2 = (bf16[8,548,1680]{2,1,0:T(8,128)(2,1)S(1)}, f32[304,512]{1,0:T(8,128)}, f32[304,512]{1,0:T(8,128)}, f32[304,512]{1,0:T(8,128)}, f32[304,512]{1,0:T(8,128)}) custom-call(f32[548,256]{1,0:T(8,128)S(1)} %copy-done.7, f32[4,304,512]{2,1,0:T(8,128)} %all-to-all-done.refs_0_), custom_call_target="tpu_custom_call" | custom-call | bytes 548 | tf_op jit(solution)/shard_map/unpack/pallas_call | solution.py:517
  79.0 2.7 %collective-permute-start.15 = (f32[548,128]{1,0:T(8,128)S(1)}, f32[548,128]{1,0:T(8,128)S(1)}, u32[]{:S(2)}, u32[]{:S(2)}) collective-permute-start(f32[548,128]{1,0:T(8,128)S(1)} %get-tuple-element.96), channel_id=1, source_target_pairs={{0,8},{24,16},{16,24},{8,0},{1,9},{25,17},{17,25},{9,1},{2,10},{26... | collective-permute-start | bytes 841736 | tf_op jit(solution)/shard_map/ppermute | solution.py:441
  87.2 3.9 %unpack.3.after.behind.g_ref = bf16[8,548,1680]{2,1,0:T(8,128)(2,1)S(1)} custom-call(f32[548,128]{1,0:T(8,128)S(1)} %get-tuple-element.91.after.refs_3_.refs_2_, f32[304,512]{1,0:T(8,128)} %copy-done.41, f32[304,512]{1,0:T(8,128)} %copy-done.42, f32[304,512]{1,0:T(8,128)} %copy-done.43, f32[304,512]{1,0:T(8,128)} %copy-done.44, ...), custom_call_target="tpu_custom_call", output_to_operand_aliasing={{}: (5, {})} | custom-call | bytes 548 | tf_op jit(solution)/shard_map/unpack/pallas_call | solution.py:517
  91.3 1.6 %collective-permute-start.17 = (f32[548,128]{1,0:T(8,128)S(1)}, f32[548,128]{1,0:T(8,128)S(1)}, u32[]{:S(2)}, u32[]{:S(2)}) collective-permute-start(f32[548,128]{1,0:T(8,128)S(1)} %get-tuple-element.105), channel_id=1, source_target_pairs={{16,24},{8,0},{17,25},{9,1},{18,26},{10,2},{19,27},{11,3},{20,28},... | collective-permute-start | bytes 841736 | tf_op jit(solution)/shard_map/ppermute | solution.py:441
  93.0 6.5 %last.4 = (f32[548,1,1024]{2,1,0:T(1,128)}, f32[548,1,1024]{2,1,0:T(1,128)}, f32[548,256]{1,0:T(8,128)S(1)}, f32[548,256]{1,0:T(8,128)S(1)}) custom-call(f32[548,128]{1,0:T(8,128)S(1)} %get-tuple-element.97.after.behind.refs_3_.refs_1_, f32[548,128]{1,0:T(8,128)S(1)} %get-tuple-element.97.after.behind.refs_3_.refs_1_, s32[1,1024]{1,0:T(1,128)S(1)} %copy-done.40, ...), custom_call_target="tpu_custom_call" | custom-call | flops 76877824 | bytes 76877824 | tf_op jit(solution)/shard_map/last/pallas_call | solution.py:580
  99.6 1.4 %collective-permute-start.18 = (f32[548,128]{1,0:T(8,128)S(1)}, f32[548,128]{1,0:T(8,128)S(1)}, u32[]{:S(2)}, u32[]{:S(2)}) collective-permute-start(f32[548,128]{1,0:T(8,128)S(1)} %get-tuple-element.110), channel_id=1, source_target_pairs={{16,24},{8,0},{17,25},{9,1},{18,26},{10,2},{19,27},{11,3},{20,28},... | collective-permute-start | bytes 841736 | tf_op jit(solution)/shard_map/ppermute | solution.py:441
  101.1 6.8 %last.5 = (f32[548,1,1024]{2,1,0:T(1,128)}, f32[548,1,1024]{2,1,0:T(1,128)}, f32[548,256]{1,0:T(8,128)S(1)}, f32[548,256]{1,0:T(8,128)S(1)}) custom-call(f32[548,128]{1,0:T(8,128)S(1)} %get-tuple-element.100.after.behind.refs_4_.refs_2_, ...), custom_call_target="tpu_custom_call", output_to_operand_aliasing={{0}: (14, {}), {1}: (15, {})} | custom-call | flops 76877824 | bytes 76877824 | tf_op jit(solution)/shard_map/last/pallas_call | solution.py:580
  107.9 6.5 %last.6 = (f32[548,1,1024]{2,1,0:T(1,128)}, f32[548,1,1024]{2,1,0:T(1,128)}, f32[548,256]{1,0:T(8,128)S(1)}, f32[548,256]{1,0:T(8,128)S(1)}) custom-call(f32[548,256]{1,0:T(8,128)S(1)} %get-tuple-element.104.after.refs_6_, f32[548,128]{1,0:T(8,128)S(1)} %collective-permute-done.17.behind.refs_3_, ...), custom_call_target="tpu_custom_call", output_to_operand_aliasing={{0}: (15, {}), {1}: (16, {})} | custom-call | flops 76877824 | bytes 76877824 | tf_op jit(solution)/shard_map/last/pallas_call | solution.py:580
  114.5 7.3 %last.7 = (f32[548,1,1024]{2,1,0:T(1,128)}, f32[548,1,1024]{2,1,0:T(1,128)}) custom-call(f32[548,256]{1,0:T(8,128)S(1)} %get-tuple-element.109.after.behind.refs_6_, f32[548,256]{1,0:T(8,128)S(1)} %get-tuple-element.109.after.behind.refs_6_, s32[1,1024]{1,0:T(1,128)S(1)} %copy-done.40, ...), custom_call_target="tpu_custom_call", output_to_operand_aliasing={{0}: (15, {}), {1}: (16, {})} | custom-call | flops 76877824 | bytes 76877824 | tf_op jit(solution)/shard_map/last/pallas_call | solution.py:580
  (133 shorter events, 18.8 us)
Async XLA Ops:
  3.4 22.4 %collective-permute-start = (f32[548,256]{1,0:T(8,128)S(1)}, f32[548,256]{1,0:T(8,128)S(1)}, u32[]{:S(2)}, u32[]{:S(2)}) collective-permute-start(f32[548,256]{1,0:T(8,128)S(1)} %first.1.after), channel_id=1, source_target_pairs={{0,8},{24,16},{1,9},{25,17},{2,10},{26,18},{3,11},{27,19},{4,12},{... | collective-permute-start | bytes 1683464 | tf_op jit(solution)/shard_map/ppermute | solution.py:441
  10.8 58.7 %all-to-all-start = ((f32[4,304,512]{2,1,0:T(8,128)}), f32[4,304,512]{2,1,0:T(8,128)}, u32[]{:S(2)}, u32[]{:S(2)}) async-start(f32[4,304,512]{2,1,0:T(8,128)} %operator.1.after), calls=%async_computation | async-start | bytes 4980736 | tf_op jit(solution)/shard_map/all_to_all | solution.py:617
  21.7 15.4 %copy-start.16 = (f32[548,256]{1,0:T(8,128)}, f32[548,256]{1,0:T(8,128)S(1)}, u32[]{:S(2)}) copy-start(f32[548,256]{1,0:T(8,128)S(1)} %get-tuple-element.60.s1_ref) | copy-start | bytes 1683460
  21.8 15.4 %copy-start.18 = (f32[548,256]{1,0:T(8,128)}, f32[548,256]{1,0:T(8,128)S(1)}, u32[]{:S(2)}) copy-start(f32[548,256]{1,0:T(8,128)S(1)} %get-tuple-element.61.s2_ref) | copy-start | bytes 1683460
  21.8 15.4 %copy-start.20 = (f32[548,256]{1,0:T(8,128)}, f32[548,256]{1,0:T(8,128)S(1)}, u32[]{:S(2)}) copy-start(f32[548,256]{1,0:T(8,128)S(1)} %get-tuple-element.62.gain_ref) | copy-start | bytes 1683460
  21.8 42.1 %copy-start = (bf16[548,1680]{1,0:T(8,128)(2,1)}, bf16[548,1680]{1,0:T(8,128)(2,1)S(1)}, u32[]{:S(2)}) copy-start(bf16[548,1680]{1,0:T(8,128)(2,1)S(1)} %get-tuple-element.63.back_ref) | copy-start | bytes 5523844
  21.8 14.5 %collective-permute-start.1 = (f32[548,256]{1,0:T(8,128)S(1)}, f32[548,256]{1,0:T(8,128)S(1)}, u32[]{:S(2)}, u32[]{:S(2)}) collective-permute-start(f32[548,256]{1,0:T(8,128)S(1)} %get-tuple-element.68), channel_id=1, source_target_pairs={{0,8},{24,16},{1,9},{25,17},{2,10},{26,18},{3,11},{27,19},{4,12},{... | collective-permute-start | bytes 1683464 | tf_op jit(solution)/shard_map/ppermute | solution.py:441
  23.1 25.3 %collective-permute-start.3 = (f32[548,256]{1,0:T(8,128)S(1)}, f32[548,256]{1,0:T(8,128)S(1)}, u32[]{:S(2)}, u32[]{:S(2)}) collective-permute-start(f32[548,256]{1,0:T(8,128)S(1)} %get-tuple-element.75), channel_id=1, source_target_pairs={{0,8},{24,16},{1,9},{25,17},{2,10},{26,18},{3,11},{27,19},{4,12},{... | collective-permute-start | bytes 1683464 | tf_op jit(solution)/shard_map/ppermute | solution.py:441
  24.4 34.6 %collective-permute-start.4 = (f32[548,256]{1,0:T(8,128)S(1)}, f32[548,256]{1,0:T(8,128)S(1)}, u32[]{:S(2)}, u32[]{:S(2)}) collective-permute-start(f32[548,256]{1,0:T(8,128)S(1)} %get-tuple-element.80), channel_id=1, source_target_pairs={{0,8},{24,16},{1,9},{25,17},{2,10},{26,18},{3,11},{27,19},{4,12},{... | collective-permute-start | bytes 1683464 | tf_op jit(solution)/shard_map/ppermute | solution.py:441
  25.9 11.2 %collective-permute-start.2 = (f32[548,256]{1,0:T(8,128)S(1)}, f32[548,256]{1,0:T(8,128)S(1)}, u32[]{:S(2)}, u32[]{:S(2)}) collective-permute-start(f32[548,256]{1,0:T(8,128)S(1)} %get-tuple-element.70), channel_id=1, source_target_pairs={{8,16},{16,8},{9,17},{17,9},{10,18},{18,10},{11,19},{19,11},{12,20... | collective-permute-start | bytes 1683464 | tf_op jit(solution)/shard_map/ppermute | solution.py:441
  36.4 24.9 %collective-permute-start.6 = (f32[548,256]{1,0:T(8,128)S(1)}, f32[548,256]{1,0:T(8,128)S(1)}, u32[]{:S(2)}, u32[]{:S(2)}) collective-permute-start(f32[548,256]{1,0:T(8,128)S(1)} %get-tuple-element.83), channel_id=1, source_target_pairs={{8,16},{16,8},{9,17},{17,9},{10,18},{18,10},{11,19},{19,11},{12,20... | collective-permute-start | bytes 1683464 | tf_op jit(solution)/shard_map/ppermute | solution.py:441
  37.3 26.6 %collective-permute-start.5 = (f32[548,256]{1,0:T(8,128)S(1)}, f32[548,256]{1,0:T(8,128)S(1)}, u32[]{:S(2)}, u32[]{:S(2)}) collective-permute-start(f32[548,256]{1,0:T(8,128)S(1)} %get-tuple-element.82), channel_id=1, source_target_pairs={{16,24},{8,0},{17,25},{9,1},{18,26},{10,2},{19,27},{11,3},{20,28},... | collective-permute-start | bytes 1683464 | tf_op jit(solution)/shard_map/ppermute | solution.py:441
  48.7 15.1 %collective-permute-start.7 = (f32[548,256]{1,0:T(8,128)S(1)}, f32[548,256]{1,0:T(8,128)S(1)}, u32[]{:S(2)}, u32[]{:S(2)}) collective-permute-start(f32[548,256]{1,0:T(8,128)S(1)} %get-tuple-element.84), channel_id=1, source_target_pairs={{8,24},{16,0},{9,25},{17,1},{10,26},{18,2},{11,27},{19,3},{12,28},... | collective-permute-start | bytes 1683464 | tf_op jit(solution)/shard_map/ppermute | solution.py:441
  60.0 15.5 %collective-permute-start.9 = (f32[548,256]{1,0:T(8,128)}, f32[548,256]{1,0:T(8,128)}, u32[]{:S(2)}, u32[]{:S(2)}) collective-permute-start(f32[548,256]{1,0:T(8,128)} %get-tuple-element.88), channel_id=1, source_target_pairs={{8,24},{16,0},{9,25},{17,1},{10,26},{18,2},{11,27},{19,3},{12,28},... | collective-permute-start | bytes 1683464 | tf_op jit(solution)/shard_map/ppermute | solution.py:441
  65.7 9.9 %collective-permute-start.8 = (f32[548,128]{1,0:T(8,128)}, f32[548,128]{1,0:T(8,128)S(1)}, u32[]{:S(2)}, u32[]{:S(2)}) collective-permute-start(f32[548,128]{1,0:T(8,128)} %get-tuple-element.87), channel_id=1, source_target_pairs={{0,8},{24,16},{16,24},{8,0},{1,9},{25,17},{17,25},{9,1},{2,10},{26... | collective-permute-start | bytes 841736 | tf_op jit(solution)/shard_map/ppermute | solution.py:441
  67.7 14.6 %collective-permute-start.10 = (f32[548,128]{1,0:T(8,128)}, f32[548,128]{1,0:T(8,128)}, u32[]{:S(2)}, u32[]{:S(2)}) collective-permute-start(f32[548,128]{1,0:T(8,128)} %get-tuple-element.90), channel_id=1, source_target_pairs={{0,8},{24,16},{16,24},{8,0},{1,9},{25,17},{17,25},{9,1},{2,10},{26... | collective-permute-start | bytes 841736 | tf_op jit(solution)/shard_map/ppermute | solution.py:441
  79.0 12.2 %collective-permute-start.15 = (f32[548,128]{1,0:T(8,128)S(1)}, f32[548,128]{1,0:T(8,128)S(1)}, u32[]{:S(2)}, u32[]{:S(2)}) collective-permute-start(f32[548,128]{1,0:T(8,128)S(1)} %get-tuple-element.96), channel_id=1, source_target_pairs={{0,8},{24,16},{16,24},{8,0},{1,9},{25,17},{17,25},{9,1},{2,10},{26... | collective-permute-start | bytes 841736 | tf_op jit(solution)/shard_map/ppermute | solution.py:441
  81.7 2.2 %collective-permute-start.11 = (f32[304,512]{1,0:T(8,128)S(1)}, f32[304,512]{1,0:T(8,128)S(1)}, u32[]{:S(2)}, u32[]{:S(2)}) collective-permute-start(f32[304,512]{1,0:T(8,128)S(1)} %copy-done.48), channel_id=1, source_target_pairs={{0,1},{1,0},{2,3},{3,2},{4,5},{5,4},{6,7},{7,6},{8,9},{9,8},{10,11... | collective-permute-start | bytes 1867784 | tf_op jit(solution)/shard_map/ppermute | solution.py:647
  81.7 3.1 %collective-permute-start.12 = (f32[304,512]{1,0:T(8,128)S(1)}, f32[304,512]{1,0:T(8,128)S(1)}, u32[]{:S(2)}, u32[]{:S(2)}) collective-permute-start(f32[304,512]{1,0:T(8,128)S(1)} %copy-done.47), channel_id=1, source_target_pairs={{0,1},{1,0},{2,3},{3,2},{4,5},{5,4},{6,7},{7,6},{8,9},{9,8},{10,11... | collective-permute-start | bytes 1867784 | tf_op jit(solution)/shard_map/ppermute | solution.py:647
  82.2 3.3 %collective-permute-start.13 = (f32[304,512]{1,0:T(8,128)S(1)}, f32[304,512]{1,0:T(8,128)S(1)}, u32[]{:S(2)}, u32[]{:S(2)}) collective-permute-start(f32[304,512]{1,0:T(8,128)S(1)} %copy-done.46), channel_id=1, source_target_pairs={{0,1},{1,0},{2,3},{3,2},{4,5},{5,4},{6,7},{7,6},{8,9},{9,8},{10,11... | collective-permute-start | bytes 1867784 | tf_op jit(solution)/shard_map/ppermute | solution.py:647
  82.3 4.1 %collective-permute-start.14 = (f32[304,512]{1,0:T(8,128)S(1)}, f32[304,512]{1,0:T(8,128)S(1)}, u32[]{:S(2)}, u32[]{:S(2)}) collective-permute-start(f32[304,512]{1,0:T(8,128)S(1)} %copy-done.45), channel_id=1, source_target_pairs={{0,1},{1,0},{2,3},{3,2},{4,5},{5,4},{6,7},{7,6},{8,9},{9,8},{10,11... | collective-permute-start | bytes 1867784 | tf_op jit(solution)/shard_map/ppermute | solution.py:647
  83.9 15.6 %collective-permute-start.16 = (f32[548,128]{1,0:T(8,128)S(1)}, f32[548,128]{1,0:T(8,128)S(1)}, u32[]{:S(2)}, u32[]{:S(2)}) collective-permute-start(f32[548,128]{1,0:T(8,128)S(1)} %get-tuple-element.99), channel_id=1, source_target_pairs={{0,8},{24,16},{16,24},{8,0},{1,9},{25,17},{17,25},{9,1},{2,10},{26... | collective-permute-start | bytes 841736 | tf_op jit(solution)/shard_map/ppermute | solution.py:441
  91.3 16.6 %collective-permute-start.17 = (f32[548,128]{1,0:T(8,128)S(1)}, f32[548,128]{1,0:T(8,128)S(1)}, u32[]{:S(2)}, u32[]{:S(2)}) collective-permute-start(f32[548,128]{1,0:T(8,128)S(1)} %get-tuple-element.105), channel_id=1, source_target_pairs={{16,24},{8,0},{17,25},{9,1},{18,26},{10,2},{19,27},{11,3},{20,28},... | collective-permute-start | bytes 841736 | tf_op jit(solution)/shard_map/ppermute | solution.py:441
  99.6 14.9 %collective-permute-start.18 = (f32[548,128]{1,0:T(8,128)S(1)}, f32[548,128]{1,0:T(8,128)S(1)}, u32[]{:S(2)}, u32[]{:S(2)}) collective-permute-start(f32[548,128]{1,0:T(8,128)S(1)} %get-tuple-element.110), channel_id=1, source_target_pairs={{16,24},{8,0},{17,25},{9,1},{18,26},{10,2},{19,27},{11,3},{20,28},... | collective-permute-start | bytes 841736 | tf_op jit(solution)/shard_map/ppermute | solution.py:441
  (45 other events, 224.6 us)

commit v2 on v1

--- a/solution.py
+++ b/solution.py
@@ -517,7 +517,7 @@
         return pl.pallas_call(
             functools.partial(unpack_kernel, int(other), size),
             out_shape=[pltpu.VMEM(shape, BF16)] + [pltpu.HBM((rows, 2 * half), F32)] * (length * (not other)),
-            in_specs=[ANY] + [HBM] * len(blocks) + [WHOLE] * other,
+            in_specs=[ANY] + [ANY if other else HBM] * len(blocks) + [WHOLE] * other,
             out_specs=[WHOLE] + [HBM] * (length * (not other)),
             scratch_shapes=[
                 pltpu.VMEM((length, rows, 2 * half), F32),
@@ -529,7 +529,7 @@
             compiler_params=params(8),
             cost_estimate=cost(0, size),
             name="unpack",
-        )(after, *map(far, blocks), *([near(before)] if other else []))
+        )(after, *map(near if other else far, blocks), *([near(before)] if other else []))
 
     def unpack_all(after):
         return pl.pallas_call(

time: 123 us -> 122 us (level)
    unnamed x98 -> x92, local copies, waits for them, and re-layouts: 5.29 us -> 4.65 us
where the time goes in v2:
time: 122 us; the launch traced here: 120 us
  Pallas kernels  52.9 us (43%)
  waiting for transfers between devices  35.3 us (29%)
  starting transfers between devices  25.8 us (21%)
  local copies, waits for them, and re-layouts  4.65 us (4%)
  between operations  1.51 us (1%)
    ppermute x15, waiting for transfers between devices, sent(): return lax.ppermute(x, 'tm', list(hops))  31.9 us
    pallas_call x4, Pallas kernels, last(): pl.pallas_call(functools.partial(last_kernel, i, depth, regions, [len(g)...  27 us
    ppermute x15, starting transfers between devices, sent(): return lax.ppermute(x, 'tm', list(hops))  19.5 us
    pallas_call x2, Pallas kernels, unpack(): pl.pallas_call(functools.partial(unpack_kernel, int(other), size), out_sh...  6.7 us
    pallas_call x1, Pallas kernels, own_operator(): pl.pallas_call(operator_kernel, out_shape=pltpu.HBM((regions // 2, rows,...  6.09 us
    pallas_call x1, Pallas kernels, rest_of(): pl.pallas_call(functools.partial(rest_kernel, pieces, depth), out_shape=[...  5.58 us
    all_to_all x1, starting transfers between devices, body(): alike = lax.all_to_all(packed, 'region', 0, 0, axis_index_groups=kinds)  5.33 us
    pallas_call x10, Pallas kernels, hop(): pl.pallas_call(functools.partial(hop_kernel, stage, depth, at, parts), ou...  4.8 us
  transfers between devices with their start and end apart: 20, of which 9 were waited for; matrix products, arithmetic and copies ran while one was open for 0% of the time, Pallas kernels for 36%

profile of v2, /device:TPU:14, one launch (start us, length us, event | category | flops | bytes accessed | tf_op | source)
XLA Modules:
  0.0 120.2 jit_solution(13368890686686901332)
XLA Ops:
  0.6 2.8 %first.1.after = f32[548,256]{1,0:T(8,128)S(1)} custom-call(f32[548,1,1024]{2,1,0:T(1,128)} %bitcast.11, f32[548,1,1024]{2,1,0:T(1,128)} %bitcast.13, f32[548,1,1024]{2,1,0:T(1,128)} %bitcast.15, f32[548,1,548]{2,1,0:T(1,128)} %bitcast.17), custom_call_target="tpu_custom_call" | custom-call | flops 461266944 | bytes 3366912 | tf_op jit(solution)/shard_map/first/pallas_call | solution.py:445
  3.4 1.3 %collective-permute-start = (f32[548,256]{1,0:T(8,128)S(1)}, f32[548,256]{1,0:T(8,128)S(1)}, u32[]{:S(2)}, u32[]{:S(2)}) collective-permute-start(f32[548,256]{1,0:T(8,128)S(1)} %first.1.after), channel_id=1, source_target_pairs={{0,8},{24,16},{1,9},{25,17},{2,10},{26,18},{3,11},{27,19},{4,12},{... | collective-permute-start | bytes 1683464 | tf_op jit(solution)/shard_map/ppermute | solution.py:441
  4.7 6.1 %operator.1.after = f32[4,304,512]{2,1,0:T(8,128)} custom-call(f32[548,256]{1,0:T(8,128)S(1)} %first.1.after, f32[548,1,1024]{2,1,0:T(1,128)} %bitcast.19, f32[1,1024]{1,0:T(1,128)} %bitcast.20, s32[1,1024]{1,0:T(1,128)} %bitcast.21), custom_call_target="tpu_custom_call" | custom-call | flops 1845067776 | bytes 4489216 | tf_op jit(solution)/shard_map/operator/pallas_call | solution.py:484
  10.8 5.3 %all-to-all-start = ((f32[4,304,512]{2,1,0:T(8,128)}), f32[4,304,512]{2,1,0:T(8,128)}, u32[]{:S(2)}, u32[]{:S(2)}) async-start(f32[4,304,512]{2,1,0:T(8,128)} %operator.1.after), calls=%async_computation | async-start | bytes 4980736 | tf_op jit(solution)/shard_map/all_to_all | solution.py:617
  16.1 5.6 %rest.1 = (bf16[548,1680]{1,0:T(8,128)(2,1)S(1)}, bf16[548,1680]{1,0:T(8,128)(2,1)S(1)}, f32[548,256]{1,0:T(8,128)S(1)}, f32[548,256]{1,0:T(8,128)}, f32[548,256...) custom-call(f32[4,304,512]{2,1,0:T(8,128)} %operator.1.after, ...), custom_call_target="tpu_custom_call" | custom-call | flops 461266944 | bytes 3366912 | tf_op jit(solution)/shard_map/rest/pallas_call | solution.py:465
  21.8 1.3 %collective-permute-start.1 = (f32[548,256]{1,0:T(8,128)S(1)}, f32[548,256]{1,0:T(8,128)S(1)}, u32[]{:S(2)}, u32[]{:S(2)}) collective-permute-start(f32[548,256]{1,0:T(8,128)S(1)} %get-tuple-element.68), channel_id=1, source_target_pairs={{0,8},{24,16},{1,9},{25,17},{2,10},{26,18},{3,11},{27,19},{4,12},{... | collective-permute-start | bytes 1683464 | tf_op jit(solution)/shard_map/ppermute | solution.py:441
  23.1 1.3 %collective-permute-start.3 = (f32[548,256]{1,0:T(8,128)S(1)}, f32[548,256]{1,0:T(8,128)S(1)}, u32[]{:S(2)}, u32[]{:S(2)}) collective-permute-start(f32[548,256]{1,0:T(8,128)S(1)} %get-tuple-element.75), channel_id=1, source_target_pairs={{0,8},{24,16},{1,9},{25,17},{2,10},{26,18},{3,11},{27,19},{4,12},{... | collective-permute-start | bytes 1683464 | tf_op jit(solution)/shard_map/ppermute | solution.py:441
  26.7 9.6 %collective-permute-done.1.in_ref = f32[548,256]{1,0:T(8,128)S(1)} collective-permute-done((f32[548,256]{1,0:T(8,128)S(1)}, f32[548,256]{1,0:T(8,128)S(1)}, u32[]{:S(2)}, u32[]{:S(2)}) %collective-permute-start.1) | collective-permute-done | bytes 561184 | tf_op jit(solution)/shard_map/ppermute | solution.py:441
  37.3 1.4 %collective-permute-start.5 = (f32[548,256]{1,0:T(8,128)S(1)}, f32[548,256]{1,0:T(8,128)S(1)}, u32[]{:S(2)}, u32[]{:S(2)}) collective-permute-start(f32[548,256]{1,0:T(8,128)S(1)} %get-tuple-element.82), channel_id=1, source_target_pairs={{16,24},{8,0},{17,25},{9,1},{18,26},{10,2},{19,27},{11,3},{20,28},... | collective-permute-start | bytes 1683464 | tf_op jit(solution)/shard_map/ppermute | solution.py:441
  38.7 9.7 %collective-permute-done.3.in_ref = f32[548,256]{1,0:T(8,128)S(1)} collective-permute-done((f32[548,256]{1,0:T(8,128)S(1)}, f32[548,256]{1,0:T(8,128)S(1)}, u32[]{:S(2)}, u32[]{:S(2)}) %collective-permute-start.3) | collective-permute-done | bytes 561184 | tf_op jit(solution)/shard_map/ppermute | solution.py:441
  48.7 1.4 %collective-permute-start.7 = (f32[548,256]{1,0:T(8,128)S(1)}, f32[548,256]{1,0:T(8,128)S(1)}, u32[]{:S(2)}, u32[]{:S(2)}) collective-permute-start(f32[548,256]{1,0:T(8,128)S(1)} %get-tuple-element.84), channel_id=1, source_target_pairs={{8,24},{16,0},{9,25},{17,1},{10,26},{18,2},{11,27},{19,3},{12,28},... | collective-permute-start | bytes 1683464 | tf_op jit(solution)/shard_map/ppermute | solution.py:441
  50.2 8.9 %collective-permute-done.4.in_ref = f32[548,256]{1,0:T(8,128)S(1)} collective-permute-done((f32[548,256]{1,0:T(8,128)S(1)}, f32[548,256]{1,0:T(8,128)S(1)}, u32[]{:S(2)}, u32[]{:S(2)}) %collective-permute-start.4) | collective-permute-done | bytes 561184 | tf_op jit(solution)/shard_map/ppermute | solution.py:441
  61.2 2.6 %collective-permute-done.5.behind.refs_2_ = f32[548,256]{1,0:T(8,128)S(1)} collective-permute-done((f32[548,256]{1,0:T(8,128)S(1)}, f32[548,256]{1,0:T(8,128)S(1)}, u32[]{:S(2)}, u32[]{:S(2)}) %collective-permute-start.5) | collective-permute-done | bytes 561184 | tf_op jit(solution)/shard_map/ppermute | solution.py:441
  65.7 1.9 %collective-permute-start.8 = (f32[548,128]{1,0:T(8,128)}, f32[548,128]{1,0:T(8,128)S(1)}, u32[]{:S(2)}, u32[]{:S(2)}) collective-permute-start(f32[548,128]{1,0:T(8,128)} %get-tuple-element.87), channel_id=1, source_target_pairs={{0,8},{24,16},{16,24},{8,0},{1,9},{25,17},{17,25},{9,1},{2,10},{26... | collective-permute-start | bytes 841736 | tf_op jit(solution)/shard_map/ppermute | solution.py:441
  67.8 1.7 %all-to-all-done.refs_0_ = f32[4,304,512]{2,1,0:T(8,128)} async-done(((f32[4,304,512]{2,1,0:T(8,128)}), f32[4,304,512]{2,1,0:T(8,128)}, u32[]{:S(2)}, u32[]{:S(2)}) %all-to-all-start) | async-done | bytes 2490400 | tf_op jit(solution)/shard_map/all_to_all | solution.py:617
  70.7 3.9 %unpack.2 = (bf16[8,548,1680]{2,1,0:T(8,128)(2,1)S(1)}, f32[304,512]{1,0:T(8,128)}, f32[304,512]{1,0:T(8,128)}, f32[304,512]{1,0:T(8,128)}, f32[304,512]{1,0:T(8,128)}) custom-call(f32[548,256]{1,0:T(8,128)S(1)} %copy-done.7, f32[4,304,512]{2,1,0:T(8,128)} %all-to-all-done.refs_0_), custom_call_target="tpu_custom_call" | custom-call | bytes 548 | tf_op jit(solution)/shard_map/unpack/pallas_call | solution.py:517
  79.0 2.7 %collective-permute-start.15 = (f32[548,128]{1,0:T(8,128)S(1)}, f32[548,128]{1,0:T(8,128)S(1)}, u32[]{:S(2)}, u32[]{:S(2)}) collective-permute-start(f32[548,128]{1,0:T(8,128)S(1)} %get-tuple-element.96), channel_id=1, source_target_pairs={{0,8},{24,16},{16,24},{8,0},{1,9},{25,17},{17,25},{9,1},{2,10},{26... | collective-permute-start | bytes 841736 | tf_op jit(solution)/shard_map/ppermute | solution.py:441
  86.4 2.8 %unpack.3.after.behind.g_ref = bf16[8,548,1680]{2,1,0:T(8,128)(2,1)S(1)} custom-call(f32[548,128]{1,0:T(8,128)S(1)} %get-tuple-element.91.after.refs_3_.refs_2_, f32[304,512]{1,0:T(8,128)S(1)} %collective-permute-done.11.refs_0_, f32[304,512]{1,0:T(8,128)S(1)} %collective-permute-done.12.refs_1_, ...), custom_call_target="tpu_custom_call", output_to_operand_aliasing={{}: (5, {})} | custom-call | bytes 548 | tf_op jit(solution)/shard_map/unpack/pallas_call | solution.py:517
  89.4 1.6 %collective-permute-start.17 = (f32[548,128]{1,0:T(8,128)S(1)}, f32[548,128]{1,0:T(8,128)S(1)}, u32[]{:S(2)}, u32[]{:S(2)}) collective-permute-start(f32[548,128]{1,0:T(8,128)S(1)} %get-tuple-element.105), channel_id=1, source_target_pairs={{16,24},{8,0},{17,25},{9,1},{18,26},{10,2},{19,27},{11,3},{20,28},... | collective-permute-start | bytes 841736 | tf_op jit(solution)/shard_map/ppermute | solution.py:441
  91.2 6.5 %last.4 = (f32[548,1,1024]{2,1,0:T(1,128)}, f32[548,1,1024]{2,1,0:T(1,128)}, f32[548,256]{1,0:T(8,128)S(1)}, f32[548,256]{1,0:T(8,128)S(1)}) custom-call(f32[548,128]{1,0:T(8,128)S(1)} %get-tuple-element.97.after.behind.refs_3_.refs_1_, f32[548,128]{1,0:T(8,128)S(1)} %get-tuple-element.97.after.behind.refs_3_.refs_1_, s32[1,1024]{1,0:T(1,128)S(1)} %copy-done.41, ...), custom_call_target="tpu_custom_call" | custom-call | flops 76877824 | bytes 76877824 | tf_op jit(solution)/shard_map/last/pallas_call | solution.py:580
  97.8 1.4 %collective-permute-start.18 = (f32[548,128]{1,0:T(8,128)S(1)}, f32[548,128]{1,0:T(8,128)S(1)}, u32[]{:S(2)}, u32[]{:S(2)}) collective-permute-start(f32[548,128]{1,0:T(8,128)S(1)} %get-tuple-element.110), channel_id=1, source_target_pairs={{16,24},{8,0},{17,25},{9,1},{18,26},{10,2},{19,27},{11,3},{20,28},... | collective-permute-start | bytes 841736 | tf_op jit(solution)/shard_map/ppermute | solution.py:441
  99.4 6.7 %last.5 = (f32[548,1,1024]{2,1,0:T(1,128)}, f32[548,1,1024]{2,1,0:T(1,128)}, f32[548,256]{1,0:T(8,128)S(1)}, f32[548,256]{1,0:T(8,128)S(1)}) custom-call(f32[548,128]{1,0:T(8,128)S(1)} %get-tuple-element.100.after.behind.refs_4_.refs_2_, ...), custom_call_target="tpu_custom_call", output_to_operand_aliasing={{0}: (14, {}), {1}: (15, {})} | custom-call | flops 76877824 | bytes 76877824 | tf_op jit(solution)/shard_map/last/pallas_call | solution.py:580
  106.2 6.5 %last.6 = (f32[548,1,1024]{2,1,0:T(1,128)}, f32[548,1,1024]{2,1,0:T(1,128)}, f32[548,256]{1,0:T(8,128)S(1)}, f32[548,256]{1,0:T(8,128)S(1)}) custom-call(f32[548,256]{1,0:T(8,128)S(1)} %get-tuple-element.104.after.refs_6_, f32[548,128]{1,0:T(8,128)S(1)} %collective-permute-done.17.behind.refs_3_, ...), custom_call_target="tpu_custom_call", output_to_operand_aliasing={{0}: (15, {}), {1}: (16, {})} | custom-call | flops 76877824 | bytes 76877824 | tf_op jit(solution)/shard_map/last/pallas_call | solution.py:580
  112.7 7.3 %last.7 = (f32[548,1,1024]{2,1,0:T(1,128)}, f32[548,1,1024]{2,1,0:T(1,128)}) custom-call(f32[548,256]{1,0:T(8,128)S(1)} %get-tuple-element.109.after.behind.refs_6_, f32[548,256]{1,0:T(8,128)S(1)} %get-tuple-element.109.after.behind.refs_6_, s32[1,1024]{1,0:T(1,128)S(1)} %copy-done.41, ...), custom_call_target="tpu_custom_call", output_to_operand_aliasing={{0}: (15, {}), {1}: (16, {})} | custom-call | flops 76877824 | bytes 76877824 | tf_op jit(solution)/shard_map/last/pallas_call | solution.py:580
  (127 shorter events, 18.2 us)
Async XLA Ops:
  3.4 22.4 %collective-permute-start = (f32[548,256]{1,0:T(8,128)S(1)}, f32[548,256]{1,0:T(8,128)S(1)}, u32[]{:S(2)}, u32[]{:S(2)}) collective-permute-start(f32[548,256]{1,0:T(8,128)S(1)} %first.1.after), channel_id=1, source_target_pairs={{0,8},{24,16},{1,9},{25,17},{2,10},{26,18},{3,11},{27,19},{4,12},{... | collective-permute-start | bytes 1683464 | tf_op jit(solution)/shard_map/ppermute | solution.py:441
  10.8 58.7 %all-to-all-start = ((f32[4,304,512]{2,1,0:T(8,128)}), f32[4,304,512]{2,1,0:T(8,128)}, u32[]{:S(2)}, u32[]{:S(2)}) async-start(f32[4,304,512]{2,1,0:T(8,128)} %operator.1.after), calls=%async_computation | async-start | bytes 4980736 | tf_op jit(solution)/shard_map/all_to_all | solution.py:617
  21.7 15.4 %copy-start.17 = (f32[548,256]{1,0:T(8,128)}, f32[548,256]{1,0:T(8,128)S(1)}, u32[]{:S(2)}) copy-start(f32[548,256]{1,0:T(8,128)S(1)} %get-tuple-element.60.s1_ref) | copy-start | bytes 1683460
  21.7 15.4 %copy-start.19 = (f32[548,256]{1,0:T(8,128)}, f32[548,256]{1,0:T(8,128)S(1)}, u32[]{:S(2)}) copy-start(f32[548,256]{1,0:T(8,128)S(1)} %get-tuple-element.61.s2_ref) | copy-start | bytes 1683460
  21.8 15.4 %copy-start.21 = (f32[548,256]{1,0:T(8,128)}, f32[548,256]{1,0:T(8,128)S(1)}, u32[]{:S(2)}) copy-start(f32[548,256]{1,0:T(8,128)S(1)} %get-tuple-element.62.gain_ref) | copy-start | bytes 1683460
  21.8 42.1 %copy-start = (bf16[548,1680]{1,0:T(8,128)(2,1)}, bf16[548,1680]{1,0:T(8,128)(2,1)S(1)}, u32[]{:S(2)}) copy-start(bf16[548,1680]{1,0:T(8,128)(2,1)S(1)} %get-tuple-element.63.back_ref) | copy-start | bytes 5523844
  21.8 14.5 %collective-permute-start.1 = (f32[548,256]{1,0:T(8,128)S(1)}, f32[548,256]{1,0:T(8,128)S(1)}, u32[]{:S(2)}, u32[]{:S(2)}) collective-permute-start(f32[548,256]{1,0:T(8,128)S(1)} %get-tuple-element.68), channel_id=1, source_target_pairs={{0,8},{24,16},{1,9},{25,17},{2,10},{26,18},{3,11},{27,19},{4,12},{... | collective-permute-start | bytes 1683464 | tf_op jit(solution)/shard_map/ppermute | solution.py:441
  23.1 25.3 %collective-permute-start.3 = (f32[548,256]{1,0:T(8,128)S(1)}, f32[548,256]{1,0:T(8,128)S(1)}, u32[]{:S(2)}, u32[]{:S(2)}) collective-permute-start(f32[548,256]{1,0:T(8,128)S(1)} %get-tuple-element.75), channel_id=1, source_target_pairs={{0,8},{24,16},{1,9},{25,17},{2,10},{26,18},{3,11},{27,19},{4,12},{... | collective-permute-start | bytes 1683464 | tf_op jit(solution)/shard_map/ppermute | solution.py:441
  24.4 34.6 %collective-permute-start.4 = (f32[548,256]{1,0:T(8,128)S(1)}, f32[548,256]{1,0:T(8,128)S(1)}, u32[]{:S(2)}, u32[]{:S(2)}) collective-permute-start(f32[548,256]{1,0:T(8,128)S(1)} %get-tuple-element.80), channel_id=1, source_target_pairs={{0,8},{24,16},{1,9},{25,17},{2,10},{26,18},{3,11},{27,19},{4,12},{... | collective-permute-start | bytes 1683464 | tf_op jit(solution)/shard_map/ppermute | solution.py:441
  25.9 11.2 %collective-permute-start.2 = (f32[548,256]{1,0:T(8,128)S(1)}, f32[548,256]{1,0:T(8,128)S(1)}, u32[]{:S(2)}, u32[]{:S(2)}) collective-permute-start(f32[548,256]{1,0:T(8,128)S(1)} %get-tuple-element.70), channel_id=1, source_target_pairs={{8,16},{16,8},{9,17},{17,9},{10,18},{18,10},{11,19},{19,11},{12,20... | collective-permute-start | bytes 1683464 | tf_op jit(solution)/shard_map/ppermute | solution.py:441
  36.4 24.8 %collective-permute-start.6 = (f32[548,256]{1,0:T(8,128)S(1)}, f32[548,256]{1,0:T(8,128)S(1)}, u32[]{:S(2)}, u32[]{:S(2)}) collective-permute-start(f32[548,256]{1,0:T(8,128)S(1)} %get-tuple-element.83), channel_id=1, source_target_pairs={{8,16},{16,8},{9,17},{17,9},{10,18},{18,10},{11,19},{19,11},{12,20... | collective-permute-start | bytes 1683464 | tf_op jit(solution)/shard_map/ppermute | solution.py:441
  37.3 26.6 %collective-permute-start.5 = (f32[548,256]{1,0:T(8,128)S(1)}, f32[548,256]{1,0:T(8,128)S(1)}, u32[]{:S(2)}, u32[]{:S(2)}) collective-permute-start(f32[548,256]{1,0:T(8,128)S(1)} %get-tuple-element.82), channel_id=1, source_target_pairs={{16,24},{8,0},{17,25},{9,1},{18,26},{10,2},{19,27},{11,3},{20,28},... | collective-permute-start | bytes 1683464 | tf_op jit(solution)/shard_map/ppermute | solution.py:441
  48.7 15.1 %collective-permute-start.7 = (f32[548,256]{1,0:T(8,128)S(1)}, f32[548,256]{1,0:T(8,128)S(1)}, u32[]{:S(2)}, u32[]{:S(2)}) collective-permute-start(f32[548,256]{1,0:T(8,128)S(1)} %get-tuple-element.84), channel_id=1, source_target_pairs={{8,24},{16,0},{9,25},{17,1},{10,26},{18,2},{11,27},{19,3},{12,28},... | collective-permute-start | bytes 1683464 | tf_op jit(solution)/shard_map/ppermute | solution.py:441
  59.9 15.5 %collective-permute-start.9 = (f32[548,256]{1,0:T(8,128)}, f32[548,256]{1,0:T(8,128)}, u32[]{:S(2)}, u32[]{:S(2)}) collective-permute-start(f32[548,256]{1,0:T(8,128)} %get-tuple-element.88), channel_id=1, source_target_pairs={{8,24},{16,0},{9,25},{17,1},{10,26},{18,2},{11,27},{19,3},{12,28},... | collective-permute-start | bytes 1683464 | tf_op jit(solution)/shard_map/ppermute | solution.py:441
  65.7 9.9 %collective-permute-start.8 = (f32[548,128]{1,0:T(8,128)}, f32[548,128]{1,0:T(8,128)S(1)}, u32[]{:S(2)}, u32[]{:S(2)}) collective-permute-start(f32[548,128]{1,0:T(8,128)} %get-tuple-element.87), channel_id=1, source_target_pairs={{0,8},{24,16},{16,24},{8,0},{1,9},{25,17},{17,25},{9,1},{2,10},{26... | collective-permute-start | bytes 841736 | tf_op jit(solution)/shard_map/ppermute | solution.py:441
  67.7 14.6 %collective-permute-start.10 = (f32[548,128]{1,0:T(8,128)}, f32[548,128]{1,0:T(8,128)}, u32[]{:S(2)}, u32[]{:S(2)}) collective-permute-start(f32[548,128]{1,0:T(8,128)} %get-tuple-element.90), channel_id=1, source_target_pairs={{0,8},{24,16},{16,24},{8,0},{1,9},{25,17},{17,25},{9,1},{2,10},{26... | collective-permute-start | bytes 841736 | tf_op jit(solution)/shard_map/ppermute | solution.py:441
  79.0 10.3 %collective-permute-start.15 = (f32[548,128]{1,0:T(8,128)S(1)}, f32[548,128]{1,0:T(8,128)S(1)}, u32[]{:S(2)}, u32[]{:S(2)}) collective-permute-start(f32[548,128]{1,0:T(8,128)S(1)} %get-tuple-element.96), channel_id=1, source_target_pairs={{0,8},{24,16},{16,24},{8,0},{1,9},{25,17},{17,25},{9,1},{2,10},{26... | collective-permute-start | bytes 841736 | tf_op jit(solution)/shard_map/ppermute | solution.py:441
  81.7 2.2 %collective-permute-start.11 = (f32[304,512]{1,0:T(8,128)S(1)}, f32[304,512]{1,0:T(8,128)S(1)}, u32[]{:S(2)}, u32[]{:S(2)}) collective-permute-start(f32[304,512]{1,0:T(8,128)S(1)} %copy-done.45), channel_id=1, source_target_pairs={{0,1},{1,0},{2,3},{3,2},{4,5},{5,4},{6,7},{7,6},{8,9},{9,8},{10,11... | collective-permute-start | bytes 1867784 | tf_op jit(solution)/shard_map/ppermute | solution.py:647
  81.7 3.1 %collective-permute-start.12 = (f32[304,512]{1,0:T(8,128)S(1)}, f32[304,512]{1,0:T(8,128)S(1)}, u32[]{:S(2)}, u32[]{:S(2)}) collective-permute-start(f32[304,512]{1,0:T(8,128)S(1)} %copy-done.44), channel_id=1, source_target_pairs={{0,1},{1,0},{2,3},{3,2},{4,5},{5,4},{6,7},{7,6},{8,9},{9,8},{10,11... | collective-permute-start | bytes 1867784 | tf_op jit(solution)/shard_map/ppermute | solution.py:647
  82.2 3.3 %collective-permute-start.13 = (f32[304,512]{1,0:T(8,128)S(1)}, f32[304,512]{1,0:T(8,128)S(1)}, u32[]{:S(2)}, u32[]{:S(2)}) collective-permute-start(f32[304,512]{1,0:T(8,128)S(1)} %copy-done.43), channel_id=1, source_target_pairs={{0,1},{1,0},{2,3},{3,2},{4,5},{5,4},{6,7},{7,6},{8,9},{9,8},{10,11... | collective-permute-start | bytes 1867784 | tf_op jit(solution)/shard_map/ppermute | solution.py:647
  82.3 4.1 %collective-permute-start.14 = (f32[304,512]{1,0:T(8,128)S(1)}, f32[304,512]{1,0:T(8,128)S(1)}, u32[]{:S(2)}, u32[]{:S(2)}) collective-permute-start(f32[304,512]{1,0:T(8,128)S(1)} %copy-done.42), channel_id=1, source_target_pairs={{0,1},{1,0},{2,3},{3,2},{4,5},{5,4},{6,7},{7,6},{8,9},{9,8},{10,11... | collective-permute-start | bytes 1867784 | tf_op jit(solution)/shard_map/ppermute | solution.py:647
  83.9 13.7 %collective-permute-start.16 = (f32[548,128]{1,0:T(8,128)S(1)}, f32[548,128]{1,0:T(8,128)S(1)}, u32[]{:S(2)}, u32[]{:S(2)}) collective-permute-start(f32[548,128]{1,0:T(8,128)S(1)} %get-tuple-element.99), channel_id=1, source_target_pairs={{0,8},{24,16},{16,24},{8,0},{1,9},{25,17},{17,25},{9,1},{2,10},{26... | collective-permute-start | bytes 841736 | tf_op jit(solution)/shard_map/ppermute | solution.py:441
  89.4 16.7 %collective-permute-start.17 = (f32[548,128]{1,0:T(8,128)S(1)}, f32[548,128]{1,0:T(8,128)S(1)}, u32[]{:S(2)}, u32[]{:S(2)}) collective-permute-start(f32[548,128]{1,0:T(8,128)S(1)} %get-tuple-element.105), channel_id=1, source_target_pairs={{16,24},{8,0},{17,25},{9,1},{18,26},{10,2},{19,27},{11,3},{20,28},... | collective-permute-start | bytes 841736 | tf_op jit(solution)/shard_map/ppermute | solution.py:441
  97.8 15.0 %collective-permute-start.18 = (f32[548,128]{1,0:T(8,128)S(1)}, f32[548,128]{1,0:T(8,128)S(1)}, u32[]{:S(2)}, u32[]{:S(2)}) collective-permute-start(f32[548,128]{1,0:T(8,128)S(1)} %get-tuple-element.110), channel_id=1, source_target_pairs={{16,24},{8,0},{17,25},{9,1},{18,26},{10,2},{19,27},{11,3},{20,28},... | collective-permute-start | bytes 841736 | tf_op jit(solution)/shard_map/ppermute | solution.py:441
  (42 other events, 219.2 us)
